TPU v7x, 768 devices: a whole 4x8x12 slice. The times are simulated.
768 devices in a mesh: dp: 48 (over z, y_hi, core), tensor: 16 (over x, y_lo).
Axes of the slice: x: 4, y: 8 (y_hi: 2, y_lo: 4; y = y_hi * 4 + y_lo), z: 12, core: 2. Of those that a mesh axis runs over, the one named last changes fastest.
Arguments:
- rows: bfloat16 [192, 128, 5120], P('dp', None, 'tensor'), may hold values from -6 to 6
- counts: int32 [48], replicated, may hold values from 1 to 4, as said below
- partner: int32 [48], replicated, may hold values from 0 to 47, as said below
- w_kv: bfloat16 [5120, 2048], P('tensor'), may hold values from -0.078125 to 0.078125
- k_gain: float32 [128], replicated, may hold values from 0.1 to 1.9
- cotangent: bfloat16 [144, 128, 2048], P('dp', None, 'tensor'), may hold values from -6 to 6
Outputs:
- keys_values: float32 [144, 128, 2048], P('dp', None, 'tensor')
- rows_grad: float32 [144, 128, 5120], P('dp', None, 'tensor')
- weight_grad: float32 [5120, 2048], P('tensor')
- gain_grad: float32 [128], replicated
Inputs may be any that keep to these rules, and one draw needn't show every extreme that they name: `counts`: half of the data indices have one live row; each of the others has 2 to 4, and some index has 4. partner pairs the data indices in two: partner[partner[d]] = d and partner[d] != d; every index with more than one live row is paired with an index with one live row, and among those the ones with more rows are paired with the ones earlier in an order fixed by the draw. Some index with 4 rows is paired with the index after it (counted round). After balancing some index has 3 live rows.
All inputs are finite; a program needn't handle non-finite values.
Results may differ from a plain program's by a relative error of at most 0.0024.
Values may be sent and summed in bfloat16 or wider, within the bound.
A program may use at most 32 MiB of HBM per device.

v0:
```python
import jax
import jax.numpy as jnp
from jax import lax
from jax.sharding import PartitionSpec as P

KV = 8


def shards(rows, counts, partner, w_kv, k_gain, cotangent):
    row_len = rows.shape[1]
    features = rows.shape[2]
    slots = cotangent.shape[0]
    own_cols = cotangent.shape[2]
    head = k_gain.shape[0]
    here = lax.axis_index("dp")
    mine = counts[here]
    other = partner[here]
    theirs = counts[other]
    out_rows = jnp.maximum(mine - theirs, 0) // 2
    in_rows = jnp.maximum(theirs - mine, 0) // 2
    keep = mine - out_rows
    new_count = keep + in_rows
    offer = lax.dynamic_index_in_dim(rows, mine - 1, 0, keepdims=True)
    piece = lax.all_gather(offer, "dp", axis=0, tiled=True)
    span = piece.shape[0]
    inside = (other >= 0) & (other < span)
    picked = lax.dynamic_index_in_dim(piece, jnp.clip(other, 0, span - 1), 0, keepdims=False)
    moved = jnp.where(inside, picked, jnp.zeros((row_len, features), jnp.bfloat16))
    position = jnp.arange(slots, dtype=jnp.int32)[:, None, None]
    balanced = jnp.where(
        position < keep,
        rows[:slots],
        jnp.where(position < new_count, moved[None], jnp.zeros_like(moved)[None]),
    )
    flat = balanced.reshape(slots * row_len, features)
    partial_kv = jnp.dot(flat, w_kv, preferred_element_type=jnp.float32)
    kv = lax.psum_scatter(partial_kv, "tensor", scatter_dimension=1, tiled=True)
    heads_here = own_cols // head
    first_head = lax.axis_index("tensor") * heads_here
    heads = kv.reshape(-1, heads_here, head)
    mean_sq = jnp.mean(heads * heads, axis=-1, keepdims=True)
    inverse = lax.rsqrt(mean_sq + 1e-06)
    normed = heads * inverse
    is_key = (first_head + jnp.arange(heads_here, dtype=jnp.int32) < KV)[None, :, None]
    token_live = jnp.repeat(jnp.arange(slots, dtype=jnp.int32) < new_count, row_len)[:, None, None]
    result = jnp.where(is_key, normed * k_gain, heads)
    keys_values = jnp.where(token_live, result, 0.0).reshape(slots, row_len, own_cols)
    grad_in = jnp.where(
        token_live, cotangent.astype(jnp.float32).reshape(-1, heads_here, head), 0.0
    )
    grad_normed = grad_in * k_gain
    grad_key = inverse * (
        grad_normed - normed * jnp.mean(grad_normed * normed, axis=-1, keepdims=True)
    )
    grad_kv = jnp.where(is_key, grad_key, grad_in).astype(jnp.bfloat16).reshape(-1, own_cols)
    gain_part = jnp.sum(jnp.where(is_key, grad_in * normed, 0.0), axis=(0, 1))
    scale = lax.rsqrt((jnp.sum(counts) * row_len).astype(jnp.float32))
    piece = lax.all_gather(grad_kv, "tensor", axis=1, tiled=True)
    grad_rows = lax.dot_general(
        piece, w_kv, (((1,), (1,)), ((), ())), preferred_element_type=jnp.float32
    )
    block = lax.dot_general(
        flat, piece, (((0,), (0,)), ((), ())), preferred_element_type=jnp.float32
    )
    grad_weight = block
    grad_rows, grad_weight = (grad_rows, grad_weight)
    weight_sum = lax.psum(grad_weight, "dp")
    gain_sum = lax.psum(gain_part, ("dp", "tensor"))
    weight_sum, gain_sum = (weight_sum, gain_sum)
    rows_grad = grad_rows.reshape(slots, row_len, features)
    return (keys_values, rows_grad, weight_sum * scale, gain_sum * scale)


def solution(mesh):
    placed = (P("dp", None, "tensor"), P(), P(), P("tensor", None), P(), P("dp", None, "tensor"))
    return jax.shard_map(
        shards,
        mesh=mesh,
        in_specs=placed,
        out_specs=(P("dp", None, "tensor"), P("dp", None, "tensor"), P("tensor", None), P()),
        check_vma=False,
    )
```

profile of v0, /device:TPU:1, one launch (start us, length us, event | category | flops | bytes accessed | tf_op | source)
XLA Modules:
  0.0 873.3 jit_solution(3929210123741582102)
XLA Ops:
  7.2 0.0 copy-start
  7.2 0.0 all-gather.3.cloned.1.call-start
  7.2 1.3 dynamic_slice.18
  10.5 1.3 fusion.10
  13.1 1.5 constant_dynamic-slice_fusion
  14.7 0.0 all-gather.3.cloned.1.call-update
  14.7 0.0 reduce-scatter.2.cloned.1.call-start
  20.0 141.6 %all-gather.3.cloned.1.call-done = bf16[48,128,320]{1,2,0:T(8,128)(2,1)} async-done(((bf16[1,128,320]{1,2,0:T(8,128)(2,1)}), bf16[48,128,320]{1,2,0:T(8,128)(2,1)}) %all-gather.3.cloned.1.call-update) | async-done | bytes 3932176 | tf_op jit(solution)/shard_map/all_gather | solution.py:24
  161.6 0.9 select_bitcast_fusion
  162.5 1.0 select_select_fusion
  163.5 0.2 copy.14
  163.7 0.0 copy-done
  163.7 2.6 fusion.11
  166.4 0.0 copy-start.2
  166.4 0.0 copy-start.4
  166.4 0.0 reduce-scatter.2.cloned.1.call-update
  166.4 0.0 all-gather.5.cloned.1.call-start
  166.5 0.1 broadcast_bitcast_fusion
  166.5 83.7 %reduce-scatter.2.cloned.1.call-done = f32[384,128]{1,0:T(8,128)} async-done(((f32[384,2048]{1,0:T(8,128)}), f32[384,128]{1,0:T(8,128)}) %reduce-scatter.2.cloned.1.call-update) | async-done | bytes 196624 | tf_op jit(solution)/shard_map/reduce_scatter | solution.py:37
  250.2 1.1 multiply_reduce_fusion
  251.3 0.0 copy-done.2
  251.3 0.0 copy-done.4
  251.3 1.2 fusion.9
  252.5 1.8 fusion.7
  254.4 0.0 all-gather.5.cloned.1.call-update
  254.4 0.0 all-reduce.2.cloned.1.call-start
  254.5 80.5 %all-gather.5.cloned.1.call-done = bf16[384,2048]{1,0:T(8,128)(2,1)} async-done(((bf16[384,128]{1,0:T(8,128)(2,1)}), bf16[384,2048]{1,0:T(8,128)(2,1)}) %all-gather.5.cloned.1.call-update) | async-done | bytes 1572880 | tf_op jit(solution)/shard_map/all_gather | solution.py:58
  335.0 3.8 fusion.13
  338.8 0.0 copy-start.3
  338.8 0.0 copy-start.1
  338.8 0.0 all-reduce.2.cloned.1.call-update
  338.8 0.6 copy-done.3
  339.4 0.6 reduce_sum.38
  340.7 120.1 %psum.15 = f32[128]{0:T(128)S(1)} all-reduce(f32[128]{0:T(128)S(1)} %get-tuple-element.16), channel_id=1, replica_groups=mesh['dp'=48,'tensor'=16] {'dp','tensor'}, use_global_device_ids=true, to_apply=%region_6.7 | all-reduce | flops 128 | bytes 1024 | tf_op jit(solution)/shard_map/psum | solution.py:68
  460.8 0.5 broadcast_multiply_fusion.2
  461.4 0.0 copy-done.1
  461.4 1.0 fusion.12
  462.4 1.0 copy.16
  463.4 399.9 %all-reduce.2.cloned.1.call-done = f32[320,2048]{1,0:T(8,128)} async-done(((f32[320,2048]{1,0:T(8,128)}), f32[320,2048]{1,0:T(8,128)}) %all-reduce.2.cloned.1.call-update) | async-done | bytes 2621456 | tf_op jit(solution)/shard_map/psum | solution.py:67
  863.3 3.5 broadcast_multiply_fusion
  (3 shorter events, 0.0 us)
Async XLA Ops:
  7.2 156.6 %copy-start = (bf16[320,2048]{1,0:T(8,128)(2,1)S(1)}, bf16[320,2048]{1,0:T(8,128)(2,1)}, u32[]{:S(2)}) copy-start(bf16[320,2048]{1,0:T(8,128)(2,1)} %param.9) | copy-start | bytes 3932164
  7.2 154.4 %all-gather.3.cloned.1.call-start = ((), (), s32[]{:S(2)}) async-start(), calls=%async_computation.1 | async-start | bytes 4014080 | tf_op jit(solution)/shard_map/all_gather | solution.py:24
  14.7 235.6 %reduce-scatter.2.cloned.1.call-start = ((), (), s32[]{:S(2)}) async-start(), calls=%async_computation.2 | async-start | bytes 3342336 | tf_op jit(solution)/shard_map/reduce_scatter | solution.py:37
  166.4 85.0 %copy-start.2 = (bf16[3,128,128]{2,1,0:T(8,128)(2,1)S(1)}, bf16[3,128,128]{2,1,0:T(8,128)(2,1)}, u32[]{:S(2)}) copy-start(bf16[3,128,128]{2,1,0:T(8,128)(2,1)} %param.11) | copy-start | bytes 294916
  166.4 85.0 %copy-start.4 = (f32[128]{0:T(128)S(1)}, f32[128]{0:T(128)}, u32[]{:S(2)}) copy-start(f32[128]{0:T(128)} %param.10) | copy-start | bytes 1540
  166.4 168.6 %all-gather.5.cloned.1.call-start = ((), (), s32[]{:S(2)}) async-start(), calls=%async_computation.3 | async-start | bytes 1671168 | tf_op jit(solution)/shard_map/all_gather | solution.py:58
  254.4 608.8 %all-reduce.2.cloned.1.call-start = ((), (), s32[]{:S(2)}) async-start(), calls=%async_computation.4 | async-start | bytes 5242880 | tf_op jit(solution)/shard_map/psum | solution.py:67
  338.8 0.7 copy-start.3
  338.8 122.6 %copy-start.1 = (bf16[384,2048]{1,0:T(8,128)(2,1)S(1)}, bf16[384,2048]{1,0:T(8,128)(2,1)}, u32[]{:S(2)}) copy-start(bf16[384,2048]{1,0:T(8,128)(2,1)} %all-gather.5.cloned.1.call-done) | copy-start | bytes 4718596
Sparse Core Ops, SparseCore 0:
  14.8 146.6 all-gather.2
  166.5 83.6 reduce-scatter.1
  254.5 80.4 all-gather.4
  338.9 524.2 all-reduce.1
where the time goes:
time: 876 us; the launch traced here: 873 us
  waiting for transfers between devices  706 us (81%)
  blocking collectives  120 us (14%)
  between operations  23 us (3%)
  other arithmetic  10.7 us (1%)
    psum x1, waiting for transfers between devices, shards(): weight_sum = lax.psum(grad_weight, 'dp')  400 us
    all_gather x1, waiting for transfers between devices, shards(): piece = lax.all_gather(offer, 'dp', axis=0, tiled=True)  142 us
    psum x1, blocking collectives, shards(): gain_sum = lax.psum(gain_part, ('dp', 'tensor'))  120 us
    reduce_scatter x1, waiting for transfers between devices, shards(): kv = lax.psum_scatter(partial_kv, 'tensor', scatter_dimension=1, tiled=True)  83.7 us
    all_gather x1, waiting for transfers between devices, shards(): piece = lax.all_gather(grad_kv, 'tensor', axis=1, tiled=True)  80.5 us
  transfers between devices with their start and end apart: 4, of which 4 were waited for; matrix products, arithmetic and copies ran while one was open for 0% of the time, Pallas kernels for 0%

commit v1 on v0

v1 whole, which is shorter than its diff:
```python
import functools

import jax
import jax.numpy as jnp
from jax import lax
from jax.experimental import pallas as pl
from jax.experimental.pallas import tpu as pltpu
from jax.sharding import PartitionSpec as P

MESH = pl.DeviceIdType.MESH
F32 = jnp.float32
BF16 = jnp.bfloat16

KV = 8
HD = 128
ROW = 128
CAP = 4
BAL = 3
NX = 4
NY = 4
NZ = 12
NDP = 48
MIDS = 24
FEAT = 320
WIDE = 2048
GROUP = 512
TILES = 14
BLOCK = 15
HALF_TILES = 160
ORDER = (0, 2, 1)
SUBS = ((0, 8), (8, 7))


def remote(src, dst, send, recv, dp, tensor):
    return pltpu.make_async_remote_copy(
        src_ref=src,
        dst_ref=dst,
        send_sem=send,
        recv_sem=recv,
        device_id=(dp, tensor),
        device_id_type=MESH,
    )


def exchange_kernel(counts, partner, rows, moved, offer, held, picked, send1, recv1, send2, recv2):
    me = lax.axis_index("dp")
    tensor = lax.axis_index("tensor")
    chip = me // 2
    is_mid = (me % 2) == (chip % 2)

    barrier = pltpu.get_barrier_semaphore()

    @pl.loop(1, NDP)
    def _(k):
        pl.semaphore_signal(barrier, inc=1, device_id=(lax.rem(me + k, NDP), tensor), device_id_type=MESH)

    last = jnp.clip(counts[me] - 1, 0, CAP - 1)
    offer[0:8] = rows[last, :, 0:128].reshape(8, 16, 128)
    offer[8:16] = rows[last, :, 128:256].reshape(8, 16, 128)
    tail = rows[last, :, 256:320]
    offer[16:24] = jnp.concatenate([tail, jnp.zeros_like(tail)], axis=1).reshape(8, 16, 128)
    pl.semaphore_wait(barrier, NDP - 1)

    def first(j):
        return remote(offer.at[j], held.at[me], send1.at[j], recv1.at[me], 2 * j + j % 2, tensor)

    @pl.loop(0, MIDS)
    def _(k):
        j = lax.rem(chip + k, MIDS)

        @pl.when(2 * j + j % 2 != me)
        def _():
            first(j).start()

    @pl.when(is_mid)
    def _():
        held[me] = offer[chip]

        @pl.loop(1, NDP)
        def _(k):
            s = lax.rem(me + k, NDP)
            remote(offer.at[0], held.at[s], send1.at[0], recv1.at[s], me, tensor).wait_recv()

        @pl.loop(1, NDP)
        def _(k):
            d = lax.rem(me + k, NDP)
            picked[d] = held[partner[d]]
            remote(picked.at[d], moved.at[chip], send2.at[d], recv2.at[chip], d, tensor).start()

        moved[chip] = held[partner[me]]

    @pl.loop(0, MIDS)
    def _(k):
        j = lax.rem(chip + k, MIDS)

        @pl.when(2 * j + j % 2 != me)
        def _():
            remote(picked.at[0], moved.at[j], send2.at[0], recv2.at[j], me, tensor).wait_recv()
            first(j).wait_send()

    @pl.when(is_mid)
    def _():
        @pl.loop(1, NDP)
        def _(k):
            d = lax.rem(me + k, NDP)
            remote(picked.at[d], moved.at[chip], send2.at[d], recv2.at[chip], d, tensor).wait_send()


def exchange(counts, partner, rows):
    vmem = pl.BlockSpec(memory_space=pltpu.VMEM)
    smem = pl.BlockSpec(memory_space=pltpu.SMEM)
    dma = pltpu.SemaphoreType.DMA
    return pl.pallas_call(
        exchange_kernel,
        out_shape=jax.ShapeDtypeStruct((MIDS, 16, 128), BF16),
        in_specs=[smem, smem, vmem],
        out_specs=vmem,
        scratch_shapes=[
            pltpu.VMEM((MIDS, 16, 128), BF16),
            pltpu.VMEM((NDP, 16, 128), BF16),
            pltpu.VMEM((NDP, 16, 128), BF16),
            dma((MIDS,)),
            dma((NDP,)),
            dma((NDP,)),
            dma((MIDS,)),
        ],
        compiler_params=pltpu.CompilerParams(
            collective_id=0, has_side_effects=True, vmem_limit_bytes=16 * 1024 * 1024
        ),
        name="row_exchange",
    )(counts, partner, rows)


def segments(head):
    out, at = [], head * 20
    end = at + 20
    while at < end:
        stop = min(end, (at // TILES + 1) * TILES)
        out.append((at, stop, (at // TILES) * BLOCK + at % TILES))
        at = stop
    return out


def main_kernel(
    counts, partner, rows, moved, w, k_gain, cot,
    kv_out, rg_out, wg_out, gain_out,
    x_all, x_t, sx, rx, acc, sy, ry, dkv, gain_all, w_away, w_core, w_own, ring_m, ring_p, y_in, ag, ag_mate,
    sx_s, rx_s, sy_s, ry_s, day_s, day_r, dax_s, dax_r, gy_s, gy_r, gx_s, gx_r,
    core_s, core_r, zm_s, zm_r, zp_s, zp_r, yh_s, yh_r, am_s, am_r, ap_s, ap_r, mate_s, mate_r,
):
    dp = lax.axis_index("dp")
    t = lax.axis_index("tensor")
    z, yh, core = dp // 4, (dp // 2) % 2, dp % 2
    x, y = t // NY, t % NY

    def dp_at(zz, hh, cc):
        return (zz * 2 + hh) * 2 + cc

    mate = dp_at(z, yh, 1 - core)
    other_y = dp_at(z, 1 - yh, core)
    up = dp_at(lax.rem(z + 1, NZ), yh, core)
    down = dp_at(lax.rem(z + NZ - 1, NZ), yh, core)

    def x_mate(k):
        return lax.rem(x + k, NX) * NY + y

    def y_mate(k):
        return x * NY + lax.rem(y + k, NY)

    barrier = pltpu.get_barrier_semaphore()
    for who in (mate, other_y, up, down):
        pl.semaphore_signal(barrier, inc=1, device_id=(who, t), device_id_type=MESH)
    for k in (1, 2, 3):
        pl.semaphore_signal(barrier, inc=1, device_id=(dp, x_mate(k)), device_id_type=MESH)
        pl.semaphore_signal(barrier, inc=1, device_id=(dp, y_mate(k)), device_id_type=MESH)

    mine = counts[dp]
    theirs = counts[partner[dp]]
    out_rows = jnp.maximum(mine - theirs, 0) // 2
    in_rows = jnp.maximum(theirs - mine, 0) // 2
    keep = mine - out_rows
    new_count = keep + in_rows

    def columns(at, size):
        return pl.ds(pl.multiple_of(at, 128), size)

    pending = []

    def go(copy):
        copy.start()
        pending.append(copy)
        return copy

    arrive_x = {}
    for n, s in enumerate(ORDER):
        own = rows[s]
        came = jnp.concatenate(
            [moved[0:8].reshape(ROW, 128), moved[8:16].reshape(ROW, 128), moved[16:24].reshape(ROW, 128)[:, :64]],
            axis=1,
        )
        own = jnp.where(s < keep, own, jnp.where(s < new_count, came, jnp.zeros_like(came)))
        x_all[s] = own
        if n == 0:
            pl.semaphore_wait(barrier, 10)
        for k in (2, 1, 3):
            to = lax.rem(x + k, NX)
            sx[s, k - 1] = jnp.dot(own, w[:, columns(to * GROUP, GROUP)], preferred_element_type=F32).astype(BF16)
            arrive_x[s, k] = go(
                remote(sx.at[s, k - 1], rx.at[s, k - 1], sx_s.at[s, k - 1], rx_s.at[s, k - 1], dp, x_mate(k))
            )
        acc[s] = jnp.dot(own, w[:, columns(x * GROUP, GROUP)], preferred_element_type=F32)

    x_t[...] = jnp.concatenate([x_all[0], x_all[1], x_all[2]], axis=0).T

    arrive_y = {}
    for s in ORDER:
        for k in (2, 1, 3):
            arrive_x[s, k].wait_recv()
        acc[s] = acc[s] + rx[s, 0].astype(F32) + rx[s, 1].astype(F32) + rx[s, 2].astype(F32)
        for k in (2, 1, 3):
            to = lax.rem(y + k, NY)
            sy[s, k - 1] = acc[s, :, columns(to * HD, HD)].astype(BF16)
            arrive_y[s, k] = go(
                remote(sy.at[s, k - 1], ry.at[s, k - 1], sy_s.at[s, k - 1], ry_s.at[s, k - 1], dp, y_mate(k))
            )

    is_key = t < KV
    gain = k_gain[...]
    gain_sum = jnp.zeros((8, HD), F32)
    arrive_dy = {}
    for s in ORDER:
        for k in (2, 1, 3):
            arrive_y[s, k].wait_recv()
        kv = acc[s, :, columns(y * HD, HD)] + ry[s, 0].astype(F32) + ry[s, 1].astype(F32) + ry[s, 2].astype(F32)
        live = s < new_count
        inverse = lax.rsqrt(jnp.mean(kv * kv, axis=-1, keepdims=True) + 1e-06)
        normed = kv * inverse
        kv_out[s] = jnp.where(live, jnp.where(is_key, normed * gain, kv), 0.0)
        g = jnp.where(live, cot[s].astype(F32), 0.0)
        gn = g * gain
        grad_key = inverse * (gn - normed * jnp.mean(gn * normed, axis=-1, keepdims=True))
        here = (pl.ds(s * ROW, ROW), columns(t * HD, HD))
        dkv[here] = jnp.where(is_key, grad_key, g).astype(BF16)
        for k in (2, 1, 3):
            arrive_dy[s, k] = go(
                remote(dkv.at[here], dkv.at[here], day_s.at[s, k - 1], day_r.at[s, k - 1], dp, y_mate(k))
            )
        gain_sum = gain_sum + jnp.sum((g * normed).reshape(ROW // 8, 8, HD), axis=0)
    gain_all[t] = jnp.where(is_key, gain_sum, 0.0)
    arrive_gy = {}
    for k in (2, 1, 3):
        arrive_gy[k] = go(remote(gain_all.at[t], gain_all.at[t], gy_s.at[k - 1], gy_r.at[k - 1], dp, y_mate(k)))

    arrive_dx = {}
    for s in ORDER:
        for k in (2, 1, 3):
            arrive_dy[s, k].wait_recv()
        here = (pl.ds(s * ROW, ROW), columns(x * GROUP, GROUP))
        for k in (2, 1, 3):
            arrive_dx[s, k] = go(
                remote(dkv.at[here], dkv.at[here], dax_s.at[s, k - 1], dax_r.at[s, k - 1], dp, x_mate(k))
            )
    arrive_gx = {}
    for k in (2, 1, 3):
        arrive_gy[k].wait_recv()
    for k in (2, 1, 3):
        here = pl.ds(x * NY, NY)
        arrive_gx[k] = go(remote(gain_all.at[here], gain_all.at[here], gx_s.at[k - 1], gx_r.at[k - 1], dp, x_mate(k)))

    for s in ORDER:
        for k in (2, 1, 3):
            arrive_dx[s, k].wait_recv()
    for k in (2, 1, 3):
        arrive_gx[k].wait_recv()

    gain_tile = jnp.concatenate([jnp.sum(gain_all[...], axis=0), jnp.zeros((8, HD), F32)], axis=0)

    def product(half, buffer, each):
        for b in range(12):
            buffer[b * BLOCK + TILES] = gain_tile
        buffer[11 * BLOCK + 6 : 11 * BLOCK + TILES] = jnp.zeros((8, 16, HD), F32)
        for q in range(2):
            value = jnp.dot(x_t[...], dkv[:, columns(half * 1024 + q * GROUP, GROUP)], preferred_element_type=F32)
            for h in range(4):
                head = q * 4 + h
                for at, stop, to in segments(head):
                    lo, hi = (at - head * 20) * 16, (stop - head * 20) * 16
                    buffer[to : to + stop - at] = value[lo:hi, h * HD : (h + 1) * HD].reshape(stop - at, 16, HD)
            each(q)

    cuts = ((0, 5 * BLOCK), (5 * BLOCK, 7 * BLOCK))
    arrive_core = []

    def send_half(q):
        at = pl.ds(*cuts[q])
        arrive_core.append(go(remote(w_away.at[at], w_core.at[at], core_s.at[q], core_r.at[q], mate, t)))

    product(1 - core, w_away, send_half)
    product(core, w_own, lambda q: None)
    for q in range(2):
        arrive_core[q].wait_recv()
        at = pl.ds(*cuts[q])
        w_own[at] = w_own[at] + w_core[at]

    def own_block(target, sub):
        return pl.ds(lax.rem(target + 2 * NZ, NZ) * BLOCK + sub[0], sub[1])

    arrive_m, arrive_p = {}, {}
    for k in range(1, 7):
        for u, sub in enumerate(SUBS):
            part = pl.ds(sub[0], sub[1])
            at = own_block(z - (7 - k), sub)
            if k == 1:
                src = w_own.at[at]
            else:
                arrive_m[k - 1, u].wait_recv()
                ring_m[k - 2, part] = ring_m[k - 2, part] + w_own[at]
                src = ring_m.at[k - 2, part]
            arrive_m[k, u] = go(
                remote(src, ring_m.at[k - 1, part], zm_s.at[k - 1, u], zm_r.at[k - 1, u], down, t)
            )
            if k > 5:
                continue
            at = own_block(z + (6 - k), sub)
            if k == 1:
                src = w_own.at[at]
            else:
                arrive_p[k - 1, u].wait_recv()
                ring_p[k - 2, part] = ring_p[k - 2, part] + w_own[at]
                src = ring_p.at[k - 2, part]
            arrive_p[k, u] = go(
                remote(src, ring_p.at[k - 1, part], zp_s.at[k - 1, u], zp_r.at[k - 1, u], up, t)
            )
        if k <= BAL:
            s = ORDER[k - 1]
            rg_out[s] = lax.dot_general(
                dkv[s * ROW : (s + 1) * ROW, :], w[...], (((1,), (1,)), ((), ())), preferred_element_type=F32
            )
    for u, sub in enumerate(SUBS):
        arrive_p[5, u].wait_recv()
        arrive_m[6, u].wait_recv()
    ring_p[4] = ring_p[4] + ring_m[5] + w_own[own_block(z, (0, BLOCK))]
    swap = go(remote(ring_p.at[4], y_in, yh_s, yh_r, other_y, t))
    swap.wait_recv()
    total = ring_p[4] + y_in[...]
    ag[pl.ds(z * TILES, TILES)] = total[:TILES].astype(BF16)
    gain_out[...] = jnp.sum(total[TILES, :8, :], axis=0, keepdims=True)

    def block(origin):
        return pl.ds(lax.rem(origin + 2 * NZ, NZ) * TILES, TILES)

    arrive_mate = []

    def to_mate(origin, n):
        at = block(origin)
        arrive_mate.append(go(remote(ag.at[at], ag_mate.at[at], mate_s.at[n], mate_r.at[n], mate, t)))

    arrive_m, arrive_p = {}, {}
    for k in range(1, 8):
        if k > 1:
            arrive_m[k - 1].wait_recv()
        if k <= 6:
            at = block(z + k - 1)
            arrive_m[k] = go(remote(ag.at[at], ag.at[at], am_s.at[k - 1], am_r.at[k - 1], down, t))
        if 1 < k <= 6:
            arrive_p[k - 1].wait_recv()
        if k <= 5:
            at = block(z - k + 1)
            arrive_p[k] = go(remote(ag.at[at], ag.at[at], ap_s.at[k - 1], ap_r.at[k - 1], up, t))
        to_mate(z + k - 1, k - 1)
        if 1 < k <= 6:
            to_mate(z - k + 1, 5 + k)
    for h in range(8):
        wg_out[:, columns(core * 1024 + h * HD, HD)] = ag[h * 20 : h * 20 + 20].reshape(FEAT, HD).astype(F32)
    for copy in arrive_mate:
        copy.wait_recv()
    for h in range(8):
        wg_out[:, columns((1 - core) * 1024 + h * HD, HD)] = ag_mate[h * 20 : h * 20 + 20].reshape(FEAT, HD).astype(F32)
    for copy in pending:
        copy.wait_send()


def main(counts, partner, rows, moved, w, k_gain, cot):
    vmem = pl.BlockSpec(memory_space=pltpu.VMEM)
    smem = pl.BlockSpec(memory_space=pltpu.SMEM)
    dma = pltpu.SemaphoreType.DMA
    V = pltpu.VMEM
    return pl.pallas_call(
        main_kernel,
        out_shape=(
            jax.ShapeDtypeStruct((BAL, ROW, HD), F32),
            jax.ShapeDtypeStruct((BAL, ROW, FEAT), F32),
            jax.ShapeDtypeStruct((FEAT, WIDE), F32),
            jax.ShapeDtypeStruct((1, HD), F32),
        ),
        in_specs=[smem, smem, vmem, vmem, vmem, vmem, vmem],
        out_specs=(vmem,) * 4,
        scratch_shapes=[
            V((BAL, ROW, FEAT), BF16),
            V((FEAT, BAL * ROW), BF16),
            V((BAL, 3, ROW, GROUP), BF16),
            V((BAL, 3, ROW, GROUP), BF16),
            V((BAL, ROW, GROUP), F32),
            V((BAL, 3, ROW, HD), BF16),
            V((BAL, 3, ROW, HD), BF16),
            V((BAL * ROW, WIDE), BF16),
            V((NX * NY, 8, HD), F32),
            V((NZ * BLOCK, 16, HD), F32),
            V((NZ * BLOCK, 16, HD), F32),
            V((NZ * BLOCK, 16, HD), F32),
            V((6, BLOCK, 16, HD), F32),
            V((5, BLOCK, 16, HD), F32),
            V((BLOCK, 16, HD), F32),
            V((NZ * TILES, 16, HD), BF16),
            V((NZ * TILES, 16, HD), BF16),
            dma((BAL, 3)), dma((BAL, 3)), dma((BAL, 3)), dma((BAL, 3)),
            dma((BAL, 3)), dma((BAL, 3)), dma((BAL, 3)), dma((BAL, 3)),
            dma((3,)), dma((3,)), dma((3,)), dma((3,)),
            dma((2,)), dma((2,)),
            dma((6, 2)), dma((6, 2)), dma((5, 2)), dma((5, 2)),
            dma(()), dma(()),
            dma((6,)), dma((6,)), dma((5,)), dma((5,)),
            dma((12,)), dma((12,)),
        ],
        compiler_params=pltpu.CompilerParams(
            collective_id=1, has_side_effects=True, vmem_limit_bytes=48 * 1024 * 1024
        ),
        name="kv_grads",
    )(counts, partner, rows, moved, w, k_gain, cot)


def shards(rows, counts, partner, w_kv, k_gain, cotangent):
    moved = exchange(counts, partner, rows)
    kv, rows_grad, weight_sum, gain_sum = main(
        counts, partner, rows, moved, w_kv, k_gain.reshape(1, HD), cotangent
    )
    scale = lax.rsqrt((jnp.sum(counts) * ROW).astype(F32))
    return kv, rows_grad, weight_sum * scale, gain_sum.reshape(HD) * scale


def solution(mesh):
    placed = (P("dp", None, "tensor"), P(), P(), P("tensor", None), P(), P("dp", None, "tensor"))
    return jax.shard_map(
        shards,
        mesh=mesh,
        in_specs=placed,
        out_specs=(P("dp", None, "tensor"), P("dp", None, "tensor"), P("tensor", None), P()),
        check_vma=False,
    )
```

time: 876 us -> 165 us (0.19)
  waiting for transfers between devices: 706 us -> 0 us
  Pallas kernels: 0 us -> 150 us
  blocking collectives: 120 us -> 0 us
  between operations: 23 us -> 1.39 us
    psum x1 -> x0, waiting for transfers between devices: 400 us -> none  [shards(): weight_sum = lax.psum(grad_weight, 'dp')]
    all_gather x2 -> x0, waiting for transfers between devices: 222 us -> none  [the longest x1 142 us: shards(): piece = lax.all_gather(offer, 'dp', axis=0, tiled=True)]
    pallas_call x0 -> x2, Pallas kernels: none -> 150 us  [the longest x1 106 us: main(): pl.pallas_call(main_kernel, out_shape=(jax.ShapeDtypeStruct((BAL, ROW, HD...]
    psum x1 -> x0, blocking collectives: 120 us -> none  [shards(): gain_sum = lax.psum(gain_part, ('dp', 'tensor'))]
    reduce_scatter x1 -> x0, waiting for transfers between devices: 83.7 us -> none  [shards(): kv = lax.psum_scatter(partial_kv, 'tensor', scatter_dimension=1, tiled=True)]
  transfers between devices with their start and end apart: 4 -> 0, of which waited for: 4 -> 0; matrix products, arithmetic and copies ran while one was open for 0% -> 0% of each run, Pallas kernels for 0% -> 0%
where the time goes in v1:
time: 165 us
  Pallas kernels  150 us (91%)
  local copies, waits for them, and re-layouts  10.2 us (6%)
  other arithmetic  2.93 us (2%)
    pallas_call x1, Pallas kernels, main(): pl.pallas_call(main_kernel, out_shape=(jax.ShapeDtypeStruct((BAL, ROW, HD...  106 us
    pallas_call x1, Pallas kernels, exchange(): pl.pallas_call(exchange_kernel, out_shape=jax.ShapeDtypeStruct((MIDS, 16,...  44.1 us
    unnamed x21, local copies, waits for them, and re-layouts  10.2 us

profile of v1, /device:TPU:1, one launch (start us, length us, event | category | flops | bytes accessed | tf_op | source)
XLA Modules:
  0.0 164.6 jit_solution(14733263442147643469)
XLA Ops:
  0.6 0.0 copy-start.7
  0.6 1.2 copy.11.rows
  1.8 0.0 copy-start.3
  1.8 0.6 copy-done.3
  2.5 0.0 copy-start.5
  2.5 0.7 copy-done.5
  3.2 44.1 %row_exchange.1.moved = bf16[24,16,128]{2,1,0:T(8,128)(2,1)S(1)} custom-call(s32[48]{0:T(128)S(1)} %copy-done.5, s32[48]{0:T(128)S(1)} %copy-done.3, bf16[4,128,320]{2,1,0:T(8,128)(2,1)S(1)} %copy.11.rows), custom_call_target="tpu_custom_call" | custom-call | tf_op jit(solution)/shard_map/row_exchange/pallas_call | solution.py:113
  47.2 0.0 copy-start
  47.2 1.3 copy-done
  48.5 0.0 copy-start.2
  48.5 0.9 copy-done.2
  49.4 0.0 copy-start.4
  49.4 0.7 copy-done.4
  50.1 0.0 copy-start.6
  50.1 0.7 copy-done.6
  50.7 0.0 copy-start.8
  50.7 0.7 copy-done.8
  51.4 106.0 %kv_grads.1 = (f32[3,128,128]{2,1,0:T(8,128)S(1)}, f32[3,128,320]{2,1,0:T(8,128)S(1)}, f32[320,2048]{1,0:T(8,128)S(1)}, f32[1,128]{1,0:T(1,128)S(1)}) custom-call(s32[48]{0:T(128)S(1)} %copy-done.6, s32[48]{0:T(128)S(1)} %copy-done.4, bf16[4,128,320]{2,1,0:T(8,128)(2,1)S(1)} %copy.11.rows, bf16[24,16,128]{2,1,0:T(8,128)(2,1)S(1)} %row_exchange.1.moved, ...), custom_call_target="tpu_custom_call" | custom-call | tf_op jit(solution)/shard_map/kv_grads/pallas_call | solution.py:388
  157.4 0.0 copy-start.1
  157.5 0.8 copy-done.1
  158.3 2.1 %copy.12 = f32[3,128,320]{1,2,0:T(8,128)} copy(f32[3,128,320]{2,1,0:T(8,128)} %copy-done.1) | data formatting | bytes 983040
  160.3 0.0 copy-done.7
  160.3 0.6 reduce_sum.9
  161.6 1.8 %broadcast_multiply_fusion = f32[320,2048]{1,0:T(8,128)} fusion(f32[320,2048]{1,0:T(8,128)S(1)} %get-tuple-element.10, f32[]{:T(128)S(6)} %rsqrt.3), kind=kLoop, calls=%fused_computation | loop fusion | flops 655360 | bytes 5242884 | tf_op jit(solution)/shard_map/mul | solution.py:438
  163.4 0.5 multiply_bitcast_fusion
  163.9 0.7 copy.14
Async XLA Ops:
  0.6 159.7 %copy-start.7 = (s32[48]{0:T(128)S(1)}, s32[48]{0:T(128)}, u32[]{:S(2)}) copy-start(s32[48]{0:T(128)} %counts.3) | copy-start | bytes 580
  1.8 0.7 copy-start.3
  2.5 0.7 copy-start.5
  47.2 1.3 copy-start
  48.5 0.9 copy-start.2
  49.4 0.7 copy-start.4
  50.1 0.7 copy-start.6
  50.7 0.7 copy-start.8
  157.4 0.8 copy-start.1

commit v2 on v1

v2 whole, which is shorter than its diff:
```python
import functools

import jax
import jax.numpy as jnp
from jax import lax
from jax.experimental import pallas as pl
from jax.experimental.pallas import tpu as pltpu
from jax.sharding import PartitionSpec as P

MESH = pl.DeviceIdType.MESH
F32 = jnp.float32
BF16 = jnp.bfloat16

KV = 8
HD = 128
ROW = 128
CAP = 4
BAL = 3
NX = 4
NY = 4
NZ = 12
NDP = 48
FEAT = 320
WIDE = 2048
GROUP = 512
TILES = 14
BLOCK = 15
HALF_TILES = 160
ORDER = (0, 2, 1)
SUBS = ((0, 7), (7, 8))
MIDS = 10
SPAN = 24


def remote(src, dst, send, recv, dp, tensor):
    return pltpu.make_async_remote_copy(
        src_ref=src,
        dst_ref=dst,
        send_sem=send,
        recv_sem=recv,
        device_id=(dp, tensor),
        device_id_type=MESH,
    )


def segments(head):
    out, at = [], head * 20
    end = at + 20
    while at < end:
        stop = min(end, (at // TILES + 1) * TILES)
        out.append((at, stop, (at // TILES) * BLOCK + at % TILES))
        at = stop
    return out


def main_kernel(
    counts, partner, rows_hbm, w_hbm, k_gain, cot_hbm,
    kv_out, rg_out, ag_out, gain_out,
    rows, w, cot, offer, held, picked, moved, x_t, sx, rx, acc, sy, ry, dkv, gain_all, w_away, w_core, w_own, ring_m, ring_p, y_in,
    sx_s, rx_s, sy_s, ry_s, day_s, day_r, dax_s, dax_r, dfx_s, dfx_r, gy_s, gy_r, gx_s, gx_r,
    load_sem, first_s, first_r, second_s, second_r,
    core_s, core_r, zm_s, zm_r, zp_s, zp_r, yh_s, yh_r, am_s, am_r, ap_s, ap_r, mate_s, mate_r,
):
    dp = lax.axis_index("dp")
    t = lax.axis_index("tensor")
    z, yh, core = dp // 4, (dp // 2) % 2, dp % 2
    x, y = t // NY, t % NY

    def dp_at(zz, hh, cc):
        return (zz * 2 + hh) * 2 + cc

    mate = dp_at(z, yh, 1 - core)
    other_y = dp_at(z, 1 - yh, core)
    up = dp_at(lax.rem(z + 1, NZ), yh, core)
    down = dp_at(lax.rem(z + NZ - 1, NZ), yh, core)
    up_two = dp_at(lax.rem(z + 2, NZ), yh, core)
    down_two = dp_at(lax.rem(z + NZ - 2, NZ), yh, core)

    chip = dp // 2
    my_mid = (chip * MIDS + SPAN - 1) // SPAN

    def mid_at(j):
        return 2 * ((j * SPAN) // MIDS) + j % 2

    is_mid = mid_at(my_mid) == dp

    def x_mate(k):
        return lax.rem(x + k, NX) * NY + y

    def y_mate(k):
        return x * NY + lax.rem(y + k, NY)

    loads = [
        pltpu.make_async_copy(src, dst, load_sem.at[n])
        for n, (src, dst) in enumerate(((rows_hbm, rows), (w_hbm, w), (cot_hbm, cot)))
    ]
    for load in loads:
        load.start()

    barrier = pltpu.get_barrier_semaphore()
    for who in (mate, other_y, up, down, up_two, down_two):
        pl.semaphore_signal(barrier, inc=1, device_id=(who, t), device_id_type=MESH)
    for k in (1, 2, 3):
        pl.semaphore_signal(barrier, inc=1, device_id=(dp, x_mate(k)), device_id_type=MESH)
        pl.semaphore_signal(barrier, inc=1, device_id=(dp, y_mate(k)), device_id_type=MESH)

    for j in range(MIDS):

        @pl.when(dp != mid_at(j))
        def _(j=j):
            pl.semaphore_signal(barrier, inc=1, device_id=(mid_at(j), t), device_id_type=MESH)

    @pl.when(is_mid)
    def _():
        @pl.loop(1, NDP)
        def _(k):
            pl.semaphore_signal(barrier, inc=1, device_id=(lax.rem(dp + k, NDP), t), device_id_type=MESH)

    mine = counts[dp]
    theirs = counts[partner[dp]]
    out_rows = jnp.maximum(mine - theirs, 0) // 2
    in_rows = jnp.maximum(theirs - mine, 0) // 2
    keep = mine - out_rows
    new_count = keep + in_rows

    def columns(at, size):
        return pl.ds(pl.multiple_of(at, 128), size)

    pending = []

    def go(copy):
        copy.start()
        pending.append(copy)
        return copy

    arrive_x, arrive_y = {}, {}

    def send_x(s, own):
        x_t[:, s * ROW : (s + 1) * ROW] = own
        flat = own.T
        for k in (2, 1, 3):
            to = lax.rem(x + k, NX)
            sx[s, k - 1] = jnp.dot(flat, w[:, columns(to * GROUP, GROUP)], preferred_element_type=F32).astype(BF16)
            arrive_x[s, k] = go(
                remote(sx.at[s, k - 1], rx.at[s, k - 1], sx_s.at[s, k - 1], rx_s.at[s, k - 1], dp, x_mate(k))
            )
        acc[s] = jnp.dot(flat, w[:, columns(x * GROUP, GROUP)], preferred_element_type=F32)

    def send_y(s):
        for k in (2, 1, 3):
            arrive_x[s, k].wait_recv()
        acc[s] = acc[s] + rx[s, 0].astype(F32) + rx[s, 1].astype(F32) + rx[s, 2].astype(F32)
        for k in (2, 1, 3):
            to = lax.rem(y + k, NY)
            sy[s, k - 1] = acc[s, :, columns(to * HD, HD)].astype(BF16)
            arrive_y[s, k] = go(
                remote(sy.at[s, k - 1], ry.at[s, k - 1], sy_s.at[s, k - 1], ry_s.at[s, k - 1], dp, y_mate(k))
            )

    def first(j):
        return remote(offer.at[j], held.at[dp], first_s.at[j], first_r.at[dp], mid_at(j), t)

    def second(j, d):
        return remote(picked.at[d], moved.at[j], second_s.at[d], second_r.at[j], d, t)

    loads[0].wait()
    offer[...] = rows[jnp.clip(mine - 1, 0, CAP - 1)].reshape(MIDS, 2, 16, HD)

    @pl.when(is_mid)
    def _():
        pl.semaphore_wait(barrier, 12 + 2 * (MIDS - 1) + NDP - MIDS)

    @pl.when(jnp.logical_not(is_mid))
    def _():
        pl.semaphore_wait(barrier, 12 + MIDS)

    for j in range(MIDS):

        @pl.when(dp != mid_at(j))
        def _(j=j):
            first(j).start()

    loads[1].wait()
    send_x(0, jnp.where(0 < keep, rows[0], jnp.zeros((FEAT, ROW), BF16)))
    send_x(2, jnp.where(2 < keep, rows[2], jnp.zeros((FEAT, ROW), BF16)))

    @pl.when(is_mid)
    def _():
        held[dp] = offer[my_mid]

        @pl.loop(1, NDP)
        def _(k):
            s = lax.rem(dp + k, NDP)
            remote(offer.at[0], held.at[s], first_s.at[0], first_r.at[s], dp, t).wait_recv()

        @pl.loop(1, NDP)
        def _(k):
            d = lax.rem(dp + k, NDP)
            picked[d] = held[partner[d]]
            second(my_mid, d).start()

        moved[my_mid] = held[partner[dp]]

    send_y(0)
    send_y(2)
    for j in range(MIDS):

        @pl.when(dp != mid_at(j))
        def _(j=j):
            second(j, 0).wait_recv()

    came = moved[...].reshape(FEAT, ROW)
    send_x(1, jnp.where(1 < keep, rows[1], jnp.where(1 < new_count, came, jnp.zeros((FEAT, ROW), BF16))))
    send_y(1)
    loads[2].wait()

    is_key = t < KV
    gain = k_gain[...]
    gain_sum = jnp.zeros((8, HD), F32)
    arrive_dy = {}
    for s in ORDER:
        for k in (2, 1, 3):
            arrive_y[s, k].wait_recv()
        kv = acc[s, :, columns(y * HD, HD)] + ry[s, 0].astype(F32) + ry[s, 1].astype(F32) + ry[s, 2].astype(F32)
        live = s < new_count
        inverse = lax.rsqrt(jnp.mean(kv * kv, axis=-1, keepdims=True) + 1e-06)
        normed = kv * inverse
        kv_out[s] = jnp.where(live, jnp.where(is_key, normed * gain, kv), 0.0)
        g = jnp.where(live, cot[s].astype(F32), 0.0)
        gn = g * gain
        grad_key = inverse * (gn - normed * jnp.mean(gn * normed, axis=-1, keepdims=True))
        here = (pl.ds(s * ROW, ROW), columns(t * HD, HD))
        dkv[here] = jnp.where(is_key, grad_key, g).astype(BF16)
        for k in (2, 1, 3):
            arrive_dy[s, k] = go(
                remote(dkv.at[here], dkv.at[here], day_s.at[s, k - 1], day_r.at[s, k - 1], dp, y_mate(k))
            )
        gain_sum = gain_sum + jnp.sum((g * normed).reshape(ROW // 8, 8, HD), axis=0)
    gain_all[t] = jnp.where(is_key, gain_sum, 0.0)
    arrive_gy = {}
    for k in (2, 1, 3):
        arrive_gy[k] = go(remote(gain_all.at[t], gain_all.at[t], gy_s.at[k - 1], gy_r.at[k - 1], dp, y_mate(k)))

    def group_rows(s, at, size, group):
        return (pl.ds(s * ROW + at, size), columns(lax.rem(group, NX) * GROUP, GROUP))

    arrive_near, arrive_far = {}, {}

    def send_near(s):
        for k in (1, 2, 3):
            arrive_dy[s, k].wait_recv()
        here = group_rows(s, 0, ROW, x)
        for k in (1, 3):
            arrive_near[s, k] = go(
                remote(dkv.at[here], dkv.at[here], dax_s.at[s, k - 1], dax_r.at[s, k - 1], dp, x_mate(k))
            )

    def send_far(s):
        for n, k in enumerate((1, 3)):
            arrive_near[s, k].wait_recv()
            here = group_rows(s, 64 * n, 64, x + NX - k)
            arrive_far[s, k] = go(
                remote(dkv.at[here], dkv.at[here], dfx_s.at[s, n], dfx_r.at[s, n], dp, x_mate(k))
            )

    def row_grad(s):
        rg_out[s] = lax.dot_general(
            w[...], dkv[s * ROW : (s + 1) * ROW, :], (((1,), (1,)), ((), ())), preferred_element_type=F32
        )

    send_near(0)
    send_near(2)
    send_far(0)
    send_near(1)
    send_far(2)
    arrive_gx = {}
    for k in (2, 1, 3):
        arrive_gy[k].wait_recv()
    for k in (2, 1, 3):
        here = pl.ds(x * NY, NY)
        arrive_gx[k] = go(remote(gain_all.at[here], gain_all.at[here], gx_s.at[k - 1], gx_r.at[k - 1], dp, x_mate(k)))
    send_far(1)
    for s in ORDER:
        for k in (1, 3):
            arrive_far[s, k].wait_recv()
        if s != ORDER[-1]:
            row_grad(s)
    for k in (2, 1, 3):
        arrive_gx[k].wait_recv()

    gain_tile = jnp.concatenate([jnp.sum(gain_all[...], axis=0), jnp.zeros((8, HD), F32)], axis=0)

    def product(half, buffer, each):
        for b in range(12):
            buffer[b * BLOCK + TILES] = gain_tile
        buffer[11 * BLOCK + 6 : 11 * BLOCK + TILES] = jnp.zeros((8, 16, HD), F32)
        for q in range(2):
            value = jnp.dot(x_t[...], dkv[:, columns(half * 1024 + q * GROUP, GROUP)], preferred_element_type=F32)
            for h in range(4):
                head = q * 4 + h
                for at, stop, to in segments(head):
                    lo, hi = (at - head * 20) * 16, (stop - head * 20) * 16
                    buffer[to : to + stop - at] = value[lo:hi, h * HD : (h + 1) * HD].reshape(stop - at, 16, HD)
            each(q)

    cuts = ((0, 5 * BLOCK), (5 * BLOCK, 7 * BLOCK))
    arrive_core = []

    def send_half(q):
        at = pl.ds(*cuts[q])
        arrive_core.append(go(remote(w_away.at[at], w_core.at[at], core_s.at[q], core_r.at[q], mate, t)))

    product(1 - core, w_away, send_half)
    product(core, w_own, lambda q: None)
    for q in range(2):
        arrive_core[q].wait_recv()
        at = pl.ds(*cuts[q])
        w_own[at] = w_own[at] + w_core[at]

    def own_block(target, sub):
        return pl.ds(lax.rem(target + 2 * NZ, NZ) * BLOCK + sub[0], sub[1])

    ways = {
        -1: (ring_m, zm_s, zm_r, down, down_two),
        1: (ring_p, zp_s, zp_r, up, up_two),
    }
    arrive = {}

    def deep(sign, u):
        return (sign < 0) == (u == 0)

    def pass_on(sign, u, d):
        ring, send_sem, recv_sem, one, two = ways[sign]
        part = pl.ds(*SUBS[u])
        own = own_block(z + sign * d, SUBS[u])
        terms = {5: (6,) if deep(sign, u) else (), 3: (5, 4), 1: (3, 2)}.get(d, ())
        for n in terms:
            arrive[sign, u, n].wait_recv()
        if terms:
            value = w_own[own]
            for n in terms:
                value = value + ring[n - 1, part]
            src = ring.at[terms[0] - 1, part]
            src[...] = value
        else:
            src = w_own.at[own]
        to = two if d in (5, 3) else one
        arrive[sign, u, d] = go(
            remote(src, ring.at[d - 1, part], send_sem.at[d - 1, u], recv_sem.at[d - 1, u], to, t)
        )

    both = ((-1, 0), (1, 0), (-1, 1), (1, 1))
    flat_first = sorted(both, key=lambda way: (deep(*way), way[1]))
    for way in both:
        pass_on(*way, 6 if deep(*way) else 5)
    for way in both:
        pass_on(*way, 4)
    row_grad(ORDER[-1])
    for way in both:
        if deep(*way):
            pass_on(*way, 5)
    for way in both:
        pass_on(*way, 2)
    for way in flat_first:
        pass_on(*way, 3)
    for way in flat_first:
        pass_on(*way, 1)
    swaps = []
    for u, sub in enumerate(SUBS):
        part = pl.ds(*sub)
        for sign in (-1, 1):
            arrive[sign, u, 1].wait_recv()
        ring_m[0, part] = ring_m[0, part] + ring_p[0, part] + w_own[own_block(z, sub)]
        swaps.append(go(remote(ring_m.at[0, part], y_in.at[part], yh_s.at[u], yh_r.at[u], other_y, t)))
    live_rows = lax.fori_loop(0, NDP, lambda d, n: n + counts[d], 0)
    scale = lax.rsqrt(jnp.full((1, HD), live_rows * ROW, jnp.int32).astype(F32))
    ag = ag_out.at[core]

    def block(origin, u):
        return pl.ds(lax.rem(origin + 2 * NZ, NZ) * TILES + 7 * u, 7)

    spread, arrive_mate, seen = {}, [], set()

    def ready(sign, u, d):
        if (sign, u, d) not in seen:
            seen.add((sign, u, d))
            spread[sign, u, d].wait_recv()

    def hand_on(sign, u, d):
        back = (d - 1) // 2 * 2
        if back:
            ready(sign, u, back)
        at = block(z - sign * back, u)
        _, _, _, one, two = ways[sign]
        send_sem, recv_sem = (am_s, am_r) if sign < 0 else (ap_s, ap_r)
        spread[sign, u, d] = go(
            remote(ag.at[at], ag.at[at], send_sem.at[d - 1, u], recv_sem.at[d - 1, u], one if d % 2 else two, t)
        )

    def to_mate(origin):
        at = pl.ds(lax.rem(origin + 2 * NZ, NZ) * TILES, TILES)
        n = len(arrive_mate)
        arrive_mate.append(go(remote(ag.at[at], ag.at[at], mate_s.at[n], mate_r.at[n], mate, t)))

    def settle(d):
        for sign in (-1, 1):
            for u in (0, 1):
                ready(sign, u, d)
            to_mate(z - sign * d)

    for u, sub in enumerate(SUBS):
        swaps[u].wait_recv()
        at = pl.ds(sub[0], 7)
        ag_out[core, block(z, u)] = ((ring_m[0, at] + y_in[at]) * scale).astype(BF16)
        for d in (2, 1):
            for sign in (-1, 1):
                hand_on(sign, u, d)
    to_mate(z)
    gain_out[...] = jnp.sum(ring_m[0, TILES, :8, :] + y_in[TILES, :8, :], axis=0, keepdims=True) * scale
    for d in (4, 3):
        for way in both:
            hand_on(*way, d)
    settle(1)
    settle(2)
    for way in both:
        if deep(*way):
            hand_on(*way, 6)
    for way in both:
        hand_on(*way, 5)
    settle(3)
    settle(4)
    settle(5)
    for way in both:
        if deep(*way):
            ready(*way, 6)
    to_mate(z + 6)
    for copy in arrive_mate:
        copy.wait_recv()
    for j in range(MIDS):

        @pl.when(dp != mid_at(j))
        def _(j=j):
            first(j).wait_send()

    @pl.when(is_mid)
    def _():
        @pl.loop(1, NDP)
        def _(k):
            second(my_mid, lax.rem(dp + k, NDP)).wait_send()

    for copy in pending:
        copy.wait_send()


def finish_kernel(kv, rg, ag, gain, kv_out, rg_out, wg_out, gain_out):
    for h in range(8):
        wg_out[:, h * HD : (h + 1) * HD] = ag[0, h * 20 : h * 20 + 20].reshape(FEAT, HD).astype(F32)

    @pl.when(pl.program_id(0) == 0)
    def _():
        kv_out[...] = kv[...]
        rg_out[...] = rg[...]
        gain_out[...] = gain[...]


def main(counts, partner, rows, w, k_gain, cot):
    vmem = pl.BlockSpec(memory_space=pltpu.VMEM)
    smem = pl.BlockSpec(memory_space=pltpu.SMEM)
    hbm = pl.BlockSpec(memory_space=pl.ANY)
    dma = pltpu.SemaphoreType.DMA
    V = pltpu.VMEM
    kv, rg, ag, gain = pl.pallas_call(
        main_kernel,
        out_shape=(
            jax.ShapeDtypeStruct((BAL, ROW, HD), F32),
            jax.ShapeDtypeStruct((BAL, FEAT, ROW), F32),
            jax.ShapeDtypeStruct((2, NZ * TILES, 16, HD), BF16),
            jax.ShapeDtypeStruct((1, HD), F32),
        ),
        in_specs=[smem, smem, hbm, hbm, vmem, hbm],
        out_specs=(vmem,) * 4,
        scratch_shapes=[
            V((CAP, FEAT, ROW), BF16),
            V((FEAT, WIDE), BF16),
            V((BAL, ROW, HD), BF16),
            V((MIDS, 2, 16, HD), BF16),
            V((NDP, 2, 16, HD), BF16),
            V((NDP, 2, 16, HD), BF16),
            V((MIDS, 2, 16, HD), BF16),
            V((FEAT, BAL * ROW), BF16),
            V((BAL, 3, ROW, GROUP), BF16),
            V((BAL, 3, ROW, GROUP), BF16),
            V((BAL, ROW, GROUP), F32),
            V((BAL, 3, ROW, HD), BF16),
            V((BAL, 3, ROW, HD), BF16),
            V((BAL * ROW, WIDE), BF16),
            V((NX * NY, 8, HD), F32),
            V((NZ * BLOCK, 16, HD), F32),
            V((NZ * BLOCK, 16, HD), F32),
            V((NZ * BLOCK, 16, HD), F32),
            V((6, BLOCK, 16, HD), F32),
            V((6, BLOCK, 16, HD), F32),
            V((BLOCK, 16, HD), F32),
            dma((BAL, 3)), dma((BAL, 3)), dma((BAL, 3)), dma((BAL, 3)),
            dma((BAL, 3)), dma((BAL, 3)), dma((BAL, 3)), dma((BAL, 3)),
            dma((BAL, 2)), dma((BAL, 2)),
            dma((3,)), dma((3,)), dma((3,)), dma((3,)),
            dma((3,)), dma((MIDS,)), dma((NDP,)), dma((NDP,)), dma((MIDS,)),
            dma((2,)), dma((2,)),
            dma((6, 2)), dma((6, 2)), dma((6, 2)), dma((6, 2)),
            dma((2,)), dma((2,)),
            dma((6, 2)), dma((6, 2)), dma((6, 2)), dma((6, 2)),
            dma((12,)), dma((12,)),
        ],
        compiler_params=pltpu.CompilerParams(
            collective_id=0, has_side_effects=True, vmem_limit_bytes=56 * 1024 * 1024
        ),
        name="kv_grads",
    )(counts, partner, rows, w, k_gain, cot)
    return pl.pallas_call(
        finish_kernel,
        grid=(2,),
        out_shape=(
            jax.ShapeDtypeStruct((BAL, ROW, HD), F32),
            jax.ShapeDtypeStruct((BAL, FEAT, ROW), F32),
            jax.ShapeDtypeStruct((FEAT, WIDE), F32),
            jax.ShapeDtypeStruct((1, HD), F32),
        ),
        in_specs=[
            pl.BlockSpec((BAL, ROW, HD), lambda i: (0, 0, 0)),
            pl.BlockSpec((BAL, FEAT, ROW), lambda i: (0, 0, 0)),
            pl.BlockSpec((1, NZ * TILES, 16, HD), lambda i: (i, 0, 0, 0)),
            pl.BlockSpec((1, HD), lambda i: (0, 0)),
        ],
        out_specs=(
            pl.BlockSpec((BAL, ROW, HD), lambda i: (0, 0, 0)),
            pl.BlockSpec((BAL, FEAT, ROW), lambda i: (0, 0, 0)),
            pl.BlockSpec((FEAT, WIDE // 2), lambda i: (0, i)),
            pl.BlockSpec((1, HD), lambda i: (0, 0)),
        ),
        compiler_params=pltpu.CompilerParams(vmem_limit_bytes=56 * 1024 * 1024),
        name="unpack",
    )(kv, rg, ag, gain)


def shards(rows, counts, partner, w_kv, k_gain, cotangent):
    kv, rows_grad, weight_grad, gain_grad = main(
        counts, partner, jnp.swapaxes(rows, 1, 2), w_kv, k_gain.reshape(1, HD), cotangent
    )
    return kv, jnp.swapaxes(rows_grad, 1, 2), weight_grad, gain_grad.reshape(HD)


def solution(mesh):
    placed = (P("dp", None, "tensor"), P(), P(), P("tensor", None), P(), P("dp", None, "tensor"))
    return jax.shard_map(
        shards,
        mesh=mesh,
        in_specs=placed,
        out_specs=(P("dp", None, "tensor"), P("dp", None, "tensor"), P("tensor", None), P()),
        check_vma=False,
    )
```

time: 165 us -> 131 us (0.79)
  Pallas kernels: 150 us -> 129 us
  local copies, waits for them, and re-layouts: 10.2 us -> 0 us
  other arithmetic: 2.93 us -> 0 us
    pallas_call x1, Pallas kernels: 44.1 us -> 3.23 us  [main(): pl.pallas_call(finish_kernel, grid=(2,), out_shape=(jax.ShapeDtypeStruct(...]
    pallas_call x1, Pallas kernels: 106 us -> 125 us  [main(): pl.pallas_call(main_kernel, out_shape=(jax.ShapeDtypeStruct((BAL, ROW, HD...]
    unnamed x21 -> x0, local copies, waits for them, and re-layouts: 10.2 us -> none
    mul x2 -> x0, other arithmetic: 2.3 us -> none  [shards(): return (kv, rows_grad, weight_sum * scale, gain_sum.reshape(HD) * scale)]
where the time goes in v2:
time: 131 us; the launch traced here: 129 us
  Pallas kernels  129 us (98%)
    pallas_call x1, Pallas kernels, main(): pl.pallas_call(main_kernel, out_shape=(jax.ShapeDtypeStruct((BAL, ROW, HD...  125 us
    pallas_call x1, Pallas kernels, main(): pl.pallas_call(finish_kernel, grid=(2,), out_shape=(jax.ShapeDtypeStruct(...  3.23 us

profile of v2, /device:TPU:1, one launch (start us, length us, event | category | flops | bytes accessed | tf_op | source)
XLA Modules:
  0.0 129.2 jit_solution(8775308373366336809)
XLA Ops:
  0.6 125.4 %kv_grads.1 = (f32[3,128,128]{2,1,0:T(8,128)}, f32[3,320,128]{2,1,0:T(8,128)}, bf16[2,168,16,128]{3,2,1,0:T(8,128)(2,1)}, f32[1,128]{1,0:T(1,128)}) custom-call(s32[48]{0:T(128)} %counts.1, s32[48]{0:T(128)} %partner.1, bf16[4,320,128]{2,1,0:T(8,128)(2,1)} %bitcast.4, bf16[320,2048]{1,0:T(8,128)(2,1)} %w_hbm.1, f32[1,128]{1,0:T(1,128)} %bitcast.5, ...), custom_call_target="tpu_custom_call" | custom-call | tf_op jit(solution)/shard_map/kv_grads/pallas_call | solution.py:472
  126.0 3.2 %unpack.1 = (f32[3,128,128]{2,1,0:T(8,128)}, f32[3,320,128]{2,1,0:T(8,128)}, f32[320,2048]{1,0:T(8,128)}, f32[1,128]{1,0:T(1,128)}) custom-call(f32[3,128,128]{2,1,0:T(8,128)} %get-tuple-element.12.kv, f32[3,320,128]{2,1,0:T(8,128)} %get-tuple-element.13.rg, bf16[2,168,16,128]{3,2,1,0:T(8,128)(2,1)} %get-tuple-element.14.ag, f32[1,128]{1,0:T(1,128)} %get-tuple-element.15.gain), custom_call_target="tpu_custom_call" | custom-call | tf_op jit(solution)/shard_map/unpack/pallas_call | solution.py:520

commit v3 on v2

--- a/solution.py
+++ b/solution.py
@@ -29,7 +29,7 @@
 ORDER = (0, 2, 1)
 SUBS = ((0, 7), (7, 8))
 MIDS = 10
-SPAN = 24
+PLACE = {0: 0, 2: 1, 1: 2}
 
 
 def remote(src, dst, send, recv, dp, tensor):
@@ -56,8 +56,8 @@
 def main_kernel(
     counts, partner, rows_hbm, w_hbm, k_gain, cot_hbm,
     kv_out, rg_out, ag_out, gain_out,
-    rows, w, cot, offer, held, picked, moved, x_t, sx, rx, acc, sy, ry, dkv, gain_all, w_away, w_core, w_own, ring_m, ring_p, y_in,
-    sx_s, rx_s, sy_s, ry_s, day_s, day_r, dax_s, dax_r, dfx_s, dfx_r, gy_s, gy_r, gx_s, gx_r,
+    rows, w, cot, offer, held, picked, moved, x_t, sx, rx, acc, sy, ry, dkv, dkv_last, sh, rh, gain_all, w_away, w_core, w_own, ring_m, ring_p, y_in,
+    sx_s, rx_s, sy_s, ry_s, hx_s, hx_r, hd_s, hd_r, day_s, day_r, dax_s, dax_r, dfx_s, dfx_r, gy_s, gy_r, gx_s, gx_r,
     load_sem, first_s, first_r, second_s, second_r,
     core_s, core_r, zm_s, zm_r, zp_s, zp_r, yh_s, yh_r, am_s, am_r, ap_s, ap_r, mate_s, mate_r,
 ):
@@ -76,13 +76,15 @@
     up_two = dp_at(lax.rem(z + 2, NZ), yh, core)
     down_two = dp_at(lax.rem(z + NZ - 2, NZ), yh, core)
 
-    chip = dp // 2
-    my_mid = (chip * MIDS + SPAN - 1) // SPAN
-
-    def mid_at(j):
-        return 2 * ((j * SPAN) // MIDS) + j % 2
-
-    is_mid = mid_at(my_mid) == dp
+    def mid_at(j, hh):
+        return dp_at(j, hh, lax.rem(j, 2))
+
+    is_mid = jnp.logical_and(z < MIDS, core == z % 2)
+    column = NDP // 2
+
+    def beside(k):
+        n = lax.rem(z * 2 + core + k, column)
+        return dp_at(n // 2, yh, n % 2)
 
     def x_mate(k):
         return lax.rem(x + k, NX) * NY + y
@@ -104,11 +106,11 @@
         pl.semaphore_signal(barrier, inc=1, device_id=(dp, x_mate(k)), device_id_type=MESH)
         pl.semaphore_signal(barrier, inc=1, device_id=(dp, y_mate(k)), device_id_type=MESH)
 
-    for j in range(MIDS):
-
-        @pl.when(dp != mid_at(j))
-        def _(j=j):
-            pl.semaphore_signal(barrier, inc=1, device_id=(mid_at(j), t), device_id_type=MESH)
+    @pl.loop(0, MIDS)
+    def _(j):
+        @pl.when(dp != mid_at(j, yh))
+        def _():
+            pl.semaphore_signal(barrier, inc=1, device_id=(mid_at(j, yh), t), device_id_type=MESH)
 
     @pl.when(is_mid)
     def _():
@@ -136,7 +138,7 @@
     arrive_x, arrive_y = {}, {}
 
     def send_x(s, own):
-        x_t[:, s * ROW : (s + 1) * ROW] = own
+        x_t[:, PLACE[s] * ROW : (PLACE[s] + 1) * ROW] = own
         flat = own.T
         for k in (2, 1, 3):
             to = lax.rem(x + k, NX)
@@ -146,39 +148,72 @@
             )
         acc[s] = jnp.dot(flat, w[:, columns(x * GROUP, GROUP)], preferred_element_type=F32)
 
+    def hop_y(s, k):
+        sy[s, k - 1] = acc[s, :, columns(lax.rem(y + k, NY) * HD, HD)].astype(BF16)
+        arrive_y[s, k] = go(
+            remote(sy.at[s, k - 1], ry.at[s, k - 1], sy_s.at[s, k - 1], ry_s.at[s, k - 1], dp, y_mate(k))
+        )
+
     def send_y(s):
         for k in (2, 1, 3):
             arrive_x[s, k].wait_recv()
         acc[s] = acc[s] + rx[s, 0].astype(F32) + rx[s, 1].astype(F32) + rx[s, 2].astype(F32)
         for k in (2, 1, 3):
-            to = lax.rem(y + k, NY)
-            sy[s, k - 1] = acc[s, :, columns(to * HD, HD)].astype(BF16)
-            arrive_y[s, k] = go(
-                remote(sy.at[s, k - 1], ry.at[s, k - 1], sy_s.at[s, k - 1], ry_s.at[s, k - 1], dp, y_mate(k))
+            hop_y(s, k)
+
+    def send_x_heads(s, own):
+        x_t[:, PLACE[s] * ROW : (PLACE[s] + 1) * ROW] = own
+        flat = own.T
+        for j in (3, 2, 1, 0):
+            head = lax.rem(y + j, NY)
+            for k in (2, 1, 3):
+                at = columns((lax.rem(x + k, NX) * NY + head) * HD, HD)
+                sh[j, k - 1] = jnp.dot(flat, w[:, at], preferred_element_type=F32).astype(BF16)
+                arrive_x[s, j, k] = go(
+                    remote(
+                        sh.at[j, k - 1], rh.at[j, k - 1], hx_s.at[j, k - 1], hx_r.at[j, k - 1], dp, x_mate(k)
+                    )
+                )
+        acc[s] = jnp.dot(flat, w[:, columns(x * GROUP, GROUP)], preferred_element_type=F32)
+
+    def send_y_heads(s):
+        for j in (3, 2, 1, 0):
+            here = columns(lax.rem(y + j, NY) * HD, HD)
+            for k in (2, 1, 3):
+                arrive_x[s, j, k].wait_recv()
+            acc[s, :, here] = (
+                acc[s, :, here] + rh[j, 0].astype(F32) + rh[j, 1].astype(F32) + rh[j, 2].astype(F32)
             )
-
-    def first(j):
-        return remote(offer.at[j], held.at[dp], first_s.at[j], first_r.at[dp], mid_at(j), t)
+            if j:
+                hop_y(s, j)
+
+    def first(j, hh):
+        return remote(offer.at[j], held.at[dp], first_s.at[hh, j], first_r.at[dp], mid_at(j, hh), t)
 
     def second(j, d):
         return remote(picked.at[d], moved.at[j], second_s.at[d], second_r.at[j], d, t)
 
+    def each_mid(act):
+        @pl.loop(0, 2 * MIDS)
+        def _(n):
+            j, hh = n // 2, n % 2
+
+            @pl.when(dp != mid_at(j, hh))
+            def _():
+                act(j, hh)
+
     loads[0].wait()
     offer[...] = rows[jnp.clip(mine - 1, 0, CAP - 1)].reshape(MIDS, 2, 16, HD)
 
     @pl.when(is_mid)
     def _():
-        pl.semaphore_wait(barrier, 12 + 2 * (MIDS - 1) + NDP - MIDS)
+        pl.semaphore_wait(barrier, 12 + 2 * MIDS - 1 + column - 1)
 
     @pl.when(jnp.logical_not(is_mid))
     def _():
-        pl.semaphore_wait(barrier, 12 + MIDS)
-
-    for j in range(MIDS):
-
-        @pl.when(dp != mid_at(j))
-        def _(j=j):
-            first(j).start()
+        pl.semaphore_wait(barrier, 12 + 2 * MIDS)
+
+    each_mid(lambda j, hh: first(j, hh).start())
 
     loads[1].wait()
     send_x(0, jnp.where(0 < keep, rows[0], jnp.zeros((FEAT, ROW), BF16)))
@@ -186,68 +221,62 @@
 
     @pl.when(is_mid)
     def _():
-        held[dp] = offer[my_mid]
+        held[dp] = offer[z]
 
         @pl.loop(1, NDP)
         def _(k):
             s = lax.rem(dp + k, NDP)
-            remote(offer.at[0], held.at[s], first_s.at[0], first_r.at[s], dp, t).wait_recv()
-
-        @pl.loop(1, NDP)
+            remote(offer.at[0], held.at[s], first_s.at[0, 0], first_r.at[s], dp, t).wait_recv()
+
+        @pl.loop(1, column)
         def _(k):
-            d = lax.rem(dp + k, NDP)
+            d = beside(k)
             picked[d] = held[partner[d]]
-            second(my_mid, d).start()
-
-        moved[my_mid] = held[partner[dp]]
-
-    send_y(0)
-    send_y(2)
-    for j in range(MIDS):
-
-        @pl.when(dp != mid_at(j))
-        def _(j=j):
-            second(j, 0).wait_recv()
-
-    came = moved[...].reshape(FEAT, ROW)
-    send_x(1, jnp.where(1 < keep, rows[1], jnp.where(1 < new_count, came, jnp.zeros((FEAT, ROW), BF16))))
-    send_y(1)
-    loads[2].wait()
+            second(z, d).start()
+
+        moved[z] = held[partner[dp]]
 
     is_key = t < KV
     gain = k_gain[...]
-    gain_sum = jnp.zeros((8, HD), F32)
-    arrive_dy = {}
-    for s in ORDER:
+    gain_parts = []
+    arrive_dy, arrive_dx, arrive_near, arrive_far = {}, {}, {}, {}
+
+    def grads(s):
+        return dkv_last if s == ORDER[-1] else dkv.at[PLACE[s] * ROW : (PLACE[s] + 1) * ROW]
+
+    def norm(s):
         for k in (2, 1, 3):
             arrive_y[s, k].wait_recv()
         kv = acc[s, :, columns(y * HD, HD)] + ry[s, 0].astype(F32) + ry[s, 1].astype(F32) + ry[s, 2].astype(F32)
         live = s < new_count
         inverse = lax.rsqrt(jnp.mean(kv * kv, axis=-1, keepdims=True) + 1e-06)
         normed = kv * inverse
-        kv_out[s] = jnp.where(live, jnp.where(is_key, normed * gain, kv), 0.0)
         g = jnp.where(live, cot[s].astype(F32), 0.0)
         gn = g * gain
         grad_key = inverse * (gn - normed * jnp.mean(gn * normed, axis=-1, keepdims=True))
-        here = (pl.ds(s * ROW, ROW), columns(t * HD, HD))
-        dkv[here] = jnp.where(is_key, grad_key, g).astype(BF16)
+        here = grads(s).at[:, columns(t * HD, HD)]
+        here[...] = jnp.where(is_key, grad_key, g).astype(BF16)
+        for k in (2, 3, 1):
+            arrive_dy[s, k] = go(
+                remote(here, here, day_s.at[s, k - 1], day_r.at[s, k - 1], dp, y_mate(k))
+            )
+        if s == ORDER[-1]:
+            send_head(s, 0)
+        kv_out[s] = jnp.where(live, jnp.where(is_key, normed * gain, kv), 0.0)
+        gain_parts.append(jnp.sum((g * normed).reshape(ROW // 8, 8, HD), axis=0))
+
+    def send_head(s, back):
+        here = grads(s).at[:, columns((x * NY + lax.rem(y + NY - back, NY)) * HD, HD)]
         for k in (2, 1, 3):
-            arrive_dy[s, k] = go(
-                remote(dkv.at[here], dkv.at[here], day_s.at[s, k - 1], day_r.at[s, k - 1], dp, y_mate(k))
+            arrive_dx[back, k] = go(
+                remote(here, here, hd_s.at[back, k - 1], hd_r.at[back, k - 1], dp, x_mate(k))
             )
-        gain_sum = gain_sum + jnp.sum((g * normed).reshape(ROW // 8, 8, HD), axis=0)
-    gain_all[t] = jnp.where(is_key, gain_sum, 0.0)
-    arrive_gy = {}
-    for k in (2, 1, 3):
-        arrive_gy[k] = go(remote(gain_all.at[t], gain_all.at[t], gy_s.at[k - 1], gy_r.at[k - 1], dp, y_mate(k)))
 
     def group_rows(s, at, size, group):
-        return (pl.ds(s * ROW + at, size), columns(lax.rem(group, NX) * GROUP, GROUP))
-
-    arrive_near, arrive_far = {}, {}
+        return (pl.ds(PLACE[s] * ROW + at, size), columns(lax.rem(group, NX) * GROUP, GROUP))
 
     def send_near(s):
-        for k in (1, 2, 3):
+        for k in (1, 3, 2):
             arrive_dy[s, k].wait_recv()
         here = group_rows(s, 0, ROW, x)
         for k in (1, 3):
@@ -264,44 +293,74 @@
             )
 
     def row_grad(s):
+        for k in (1, 3):
+            if (s, k) in arrive_far:
+                arrive_far[s, k].wait_recv()
         rg_out[s] = lax.dot_general(
-            w[...], dkv[s * ROW : (s + 1) * ROW, :], (((1,), (1,)), ((), ())), preferred_element_type=F32
+            w[...], grads(s)[...], (((1,), (1,)), ((), ())), preferred_element_type=F32
         )
 
+    send_y(0)
+    send_y(2)
+    loads[2].wait()
+    norm(0)
+
+    @pl.loop(0, MIDS)
+    def _(j):
+        @pl.when(dp != mid_at(j, yh))
+        def _():
+            second(j, dp).wait_recv()
+
+    came = moved[...].reshape(FEAT, ROW)
+    send_x_heads(1, jnp.where(1 < keep, rows[1], jnp.where(1 < new_count, came, jnp.zeros((FEAT, ROW), BF16))))
+    norm(2)
     send_near(0)
     send_near(2)
+    send_y_heads(1)
     send_far(0)
-    send_near(1)
     send_far(2)
-    arrive_gx = {}
+    norm(1)
+    gain_all[t] = jnp.where(is_key, gain_parts[0] + gain_parts[1] + gain_parts[2], 0.0)
+    arrive_gy, arrive_gx = {}, {}
     for k in (2, 1, 3):
+        arrive_gy[k] = go(remote(gain_all.at[t], gain_all.at[t], gy_s.at[k - 1], gy_r.at[k - 1], dp, y_mate(k)))
+    row_grad(0)
+    for k in (1, 3, 2):
+        arrive_dy[1, k].wait_recv()
+        send_head(1, k)
+    for k in (1, 3, 2):
         arrive_gy[k].wait_recv()
     for k in (2, 1, 3):
         here = pl.ds(x * NY, NY)
         arrive_gx[k] = go(remote(gain_all.at[here], gain_all.at[here], gx_s.at[k - 1], gx_r.at[k - 1], dp, x_mate(k)))
-    send_far(1)
-    for s in ORDER:
-        for k in (1, 3):
-            arrive_far[s, k].wait_recv()
-        if s != ORDER[-1]:
-            row_grad(s)
-    for k in (2, 1, 3):
-        arrive_gx[k].wait_recv()
-
-    gain_tile = jnp.concatenate([jnp.sum(gain_all[...], axis=0), jnp.zeros((8, HD), F32)], axis=0)
-
-    def product(half, buffer, each):
-        for b in range(12):
-            buffer[b * BLOCK + TILES] = gain_tile
-        buffer[11 * BLOCK + 6 : 11 * BLOCK + TILES] = jnp.zeros((8, 16, HD), F32)
+    row_grad(2)
+
+    def product(half, buffer, rows_at, grad, add, each):
         for q in range(2):
-            value = jnp.dot(x_t[...], dkv[:, columns(half * 1024 + q * GROUP, GROUP)], preferred_element_type=F32)
+            value = jnp.dot(
+                x_t[:, rows_at], grad[:, columns(half * 1024 + q * GROUP, GROUP)], preferred_element_type=F32
+            )
             for h in range(4):
                 head = q * 4 + h
                 for at, stop, to in segments(head):
                     lo, hi = (at - head * 20) * 16, (stop - head * 20) * 16
-                    buffer[to : to + stop - at] = value[lo:hi, h * HD : (h + 1) * HD].reshape(stop - at, 16, HD)
+                    tiles = value[lo:hi, h * HD : (h + 1) * HD].reshape(stop - at, 16, HD)
+                    buffer[to : to + stop - at] = buffer[to : to + stop - at] + tiles if add else tiles
             each(q)
+
+    early, late = slice(0, 2 * ROW), slice(2 * ROW, 3 * ROW)
+    product(1 - core, w_away, early, dkv, False, lambda q: None)
+    product(core, w_own, early, dkv, False, lambda q: None)
+    for k in (2, 1, 3):
+        arrive_gx[k].wait_recv()
+    gain_tile = jnp.concatenate([jnp.sum(gain_all[...], axis=0), jnp.zeros((8, HD), F32)], axis=0)
+    for buffer in (w_away, w_own):
+        for b in range(12):
+            buffer[b * BLOCK + TILES] = gain_tile
+        buffer[11 * BLOCK + 6 : 11 * BLOCK + TILES] = jnp.zeros((8, 16, HD), F32)
+    for back in (0, 1, 3, 2):
+        for k in (2, 1, 3):
+            arrive_dx[back, k].wait_recv()
 
     cuts = ((0, 5 * BLOCK), (5 * BLOCK, 7 * BLOCK))
     arrive_core = []
@@ -310,8 +369,8 @@
         at = pl.ds(*cuts[q])
         arrive_core.append(go(remote(w_away.at[at], w_core.at[at], core_s.at[q], core_r.at[q], mate, t)))
 
-    product(1 - core, w_away, send_half)
-    product(core, w_own, lambda q: None)
+    product(1 - core, w_away, late, dkv_last, True, send_half)
+    product(core, w_own, late, dkv_last, True, lambda q: None)
     for q in range(2):
         arrive_core[q].wait_recv()
         at = pl.ds(*cuts[q])
@@ -436,17 +495,13 @@
     to_mate(z + 6)
     for copy in arrive_mate:
         copy.wait_recv()
-    for j in range(MIDS):
-
-        @pl.when(dp != mid_at(j))
-        def _(j=j):
-            first(j).wait_send()
+    each_mid(lambda j, hh: first(j, hh).wait_send())
 
     @pl.when(is_mid)
     def _():
-        @pl.loop(1, NDP)
+        @pl.loop(1, column)
         def _(k):
-            second(my_mid, lax.rem(dp + k, NDP)).wait_send()
+            second(z, beside(k)).wait_send()
 
     for copy in pending:
         copy.wait_send()
@@ -493,7 +548,10 @@
             V((BAL, ROW, GROUP), F32),
             V((BAL, 3, ROW, HD), BF16),
             V((BAL, 3, ROW, HD), BF16),
-            V((BAL * ROW, WIDE), BF16),
+            V((2 * ROW, WIDE), BF16),
+            V((ROW, WIDE), BF16),
+            V((4, 3, ROW, HD), BF16),
+            V((4, 3, ROW, HD), BF16),
             V((NX * NY, 8, HD), F32),
             V((NZ * BLOCK, 16, HD), F32),
             V((NZ * BLOCK, 16, HD), F32),
@@ -502,10 +560,11 @@
             V((6, BLOCK, 16, HD), F32),
             V((BLOCK, 16, HD), F32),
             dma((BAL, 3)), dma((BAL, 3)), dma((BAL, 3)), dma((BAL, 3)),
+            dma((4, 3)), dma((4, 3)), dma((4, 3)), dma((4, 3)),
             dma((BAL, 3)), dma((BAL, 3)), dma((BAL, 3)), dma((BAL, 3)),
             dma((BAL, 2)), dma((BAL, 2)),
             dma((3,)), dma((3,)), dma((3,)), dma((3,)),
-            dma((3,)), dma((MIDS,)), dma((NDP,)), dma((NDP,)), dma((MIDS,)),
+            dma((3,)), dma((2, MIDS)), dma((NDP,)), dma((NDP,)), dma((MIDS,)),
             dma((2,)), dma((2,)),
             dma((6, 2)), dma((6, 2)), dma((6, 2)), dma((6, 2)),
             dma((2,)), dma((2,)),

time: 131 us -> 122 us (0.931)
  Pallas kernels: 129 us -> 120 us
    pallas_call x1, Pallas kernels: 125 us -> 117 us  [main(): pl.pallas_call(main_kernel, out_shape=(jax.ShapeDtypeStruct((BAL, ROW, HD...]
where the time goes in v3:
time: 122 us; the launch traced here: 121 us
  Pallas kernels  120 us (98%)
    pallas_call x1, Pallas kernels, main(): pl.pallas_call(main_kernel, out_shape=(jax.ShapeDtypeStruct((BAL, ROW, HD...  117 us
    pallas_call x1, Pallas kernels, main(): pl.pallas_call(finish_kernel, grid=(2,), out_shape=(jax.ShapeDtypeStruct(...  3.23 us

profile of v3, /device:TPU:1, one launch (start us, length us, event | category | flops | bytes accessed | tf_op | source)
XLA Modules:
  0.0 121.0 jit_solution(3780938520514747805)
XLA Ops:
  0.6 117.2 %kv_grads.1 = (f32[3,128,128]{2,1,0:T(8,128)}, f32[3,320,128]{2,1,0:T(8,128)}, bf16[2,168,16,128]{3,2,1,0:T(8,128)(2,1)}, f32[1,128]{1,0:T(1,128)}) custom-call(s32[48]{0:T(128)} %counts.1, s32[48]{0:T(128)} %partner.1, bf16[4,320,128]{2,1,0:T(8,128)(2,1)} %bitcast.4, bf16[320,2048]{1,0:T(8,128)(2,1)} %w_hbm.1, f32[1,128]{1,0:T(1,128)} %bitcast.5, ...), custom_call_target="tpu_custom_call" | custom-call | tf_op jit(solution)/shard_map/kv_grads/pallas_call | solution.py:527
  117.8 3.2 %unpack.1 = (f32[3,128,128]{2,1,0:T(8,128)}, f32[3,320,128]{2,1,0:T(8,128)}, f32[320,2048]{1,0:T(8,128)}, f32[1,128]{1,0:T(1,128)}) custom-call(f32[3,128,128]{2,1,0:T(8,128)} %get-tuple-element.12.kv, f32[3,320,128]{2,1,0:T(8,128)} %get-tuple-element.13.rg, bf16[2,168,16,128]{3,2,1,0:T(8,128)(2,1)} %get-tuple-element.14.ag, f32[1,128]{1,0:T(1,128)} %get-tuple-element.15.gain), custom_call_target="tpu_custom_call" | custom-call | tf_op jit(solution)/shard_map/unpack/pallas_call | solution.py:579

commit v4 on v3

--- a/solution.py
+++ b/solution.py
@@ -56,7 +56,7 @@
 def main_kernel(
     counts, partner, rows_hbm, w_hbm, k_gain, cot_hbm,
     kv_out, rg_out, ag_out, gain_out,
-    rows, w, cot, offer, held, picked, moved, x_t, sx, rx, acc, sy, ry, dkv, dkv_last, sh, rh, gain_all, w_away, w_core, w_own, ring_m, ring_p, y_in,
+    rows, w, cot, offer, held, picked, moved, x_t, sx, rx, acc, sy, ry, dkv, dkv_last, sh, rh, gain_all, w_away, w_core, w_own, ring_m, ring_p, leaf_s, leaf_r, y_in,
     sx_s, rx_s, sy_s, ry_s, hx_s, hx_r, hd_s, hd_r, day_s, day_r, dax_s, dax_r, dfx_s, dfx_r, gy_s, gy_r, gx_s, gx_r,
     load_sem, first_s, first_r, second_s, second_r,
     core_s, core_r, zm_s, zm_r, zp_s, zp_r, yh_s, yh_r, am_s, am_r, ap_s, ap_r, mate_s, mate_r,
@@ -217,7 +217,6 @@
 
     loads[1].wait()
     send_x(0, jnp.where(0 < keep, rows[0], jnp.zeros((FEAT, ROW), BF16)))
-    send_x(2, jnp.where(2 < keep, rows[2], jnp.zeros((FEAT, ROW), BF16)))
 
     @pl.when(is_mid)
     def _():
@@ -235,6 +234,8 @@
             second(z, d).start()
 
         moved[z] = held[partner[dp]]
+
+    send_x(2, jnp.where(2 < keep, rows[2], jnp.zeros((FEAT, ROW), BF16)))
 
     is_key = t < KV
     gain = k_gain[...]
@@ -388,6 +389,12 @@
     def deep(sign, u):
         return (sign < 0) == (u == 0)
 
+    def ends(sign, u, d):
+        return d in (6, 4, 2) or (d == 5 and not deep(sign, u))
+
+    def leaf(sign, d):
+        return (0 if sign < 0 else 3) + {6: 0, 5: 0, 4: 1, 2: 2}[d]
+
     def pass_on(sign, u, d):
         ring, send_sem, recv_sem, one, two = ways[sign]
         part = pl.ds(*SUBS[u])
@@ -395,18 +402,22 @@
         terms = {5: (6,) if deep(sign, u) else (), 3: (5, 4), 1: (3, 2)}.get(d, ())
         for n in terms:
             arrive[sign, u, n].wait_recv()
+        value = w_own[own]
         if terms:
-            value = w_own[own]
             for n in terms:
-                value = value + ring[n - 1, part]
-            src = ring.at[terms[0] - 1, part]
+                value = value + (leaf_r[leaf(sign, n), part].astype(F32) if ends(sign, u, n) else ring[n - 1, part])
+            src, dst = ring.at[terms[0] - 1, part], ring.at[d - 1, part]
             src[...] = value
         else:
-            src = w_own.at[own]
+            at = leaf(sign, d)
+            src, dst = leaf_s.at[at, part], leaf_r.at[at, part]
+            src[...] = value.astype(BF16)
+            if u == 1:
+                high = value[7, :8].astype(BF16)
+                low = (value[7, :8] - high.astype(F32)).astype(BF16)
+                leaf_s[at, TILES] = jnp.concatenate([high, low], axis=0)
         to = two if d in (5, 3) else one
-        arrive[sign, u, d] = go(
-            remote(src, ring.at[d - 1, part], send_sem.at[d - 1, u], recv_sem.at[d - 1, u], to, t)
-        )
+        arrive[sign, u, d] = go(remote(src, dst, send_sem.at[d - 1, u], recv_sem.at[d - 1, u], to, t))
 
     both = ((-1, 0), (1, 0), (-1, 1), (1, 1))
     flat_first = sorted(both, key=lambda way: (deep(*way), way[1]))
@@ -475,7 +486,7 @@
             for sign in (-1, 1):
                 hand_on(sign, u, d)
     to_mate(z)
-    gain_out[...] = jnp.sum(ring_m[0, TILES, :8, :] + y_in[TILES, :8, :], axis=0, keepdims=True) * scale
+    gain_out[...] = jnp.sum(ring_m[0, TILES] + y_in[TILES], axis=0, keepdims=True) * scale
     for d in (4, 3):
         for way in both:
             hand_on(*way, d)
@@ -508,7 +519,7 @@
 
 
 def finish_kernel(kv, rg, ag, gain, kv_out, rg_out, wg_out, gain_out):
-    for h in range(8):
+    for h in range(4):
         wg_out[:, h * HD : (h + 1) * HD] = ag[0, h * 20 : h * 20 + 20].reshape(FEAT, HD).astype(F32)
 
     @pl.when(pl.program_id(0) == 0)
@@ -558,6 +569,8 @@
             V((NZ * BLOCK, 16, HD), F32),
             V((6, BLOCK, 16, HD), F32),
             V((6, BLOCK, 16, HD), F32),
+            V((6, BLOCK, 16, HD), BF16),
+            V((6, BLOCK, 16, HD), BF16),
             V((BLOCK, 16, HD), F32),
             dma((BAL, 3)), dma((BAL, 3)), dma((BAL, 3)), dma((BAL, 3)),
             dma((4, 3)), dma((4, 3)), dma((4, 3)), dma((4, 3)),
@@ -578,7 +591,7 @@
     )(counts, partner, rows, w, k_gain, cot)
     return pl.pallas_call(
         finish_kernel,
-        grid=(2,),
+        grid=(4,),
         out_shape=(
             jax.ShapeDtypeStruct((BAL, ROW, HD), F32),
             jax.ShapeDtypeStruct((BAL, FEAT, ROW), F32),
@@ -588,13 +601,13 @@
         in_specs=[
             pl.BlockSpec((BAL, ROW, HD), lambda i: (0, 0, 0)),
             pl.BlockSpec((BAL, FEAT, ROW), lambda i: (0, 0, 0)),
-            pl.BlockSpec((1, NZ * TILES, 16, HD), lambda i: (i, 0, 0, 0)),
+            pl.BlockSpec((1, HALF_TILES // 2, 16, HD), lambda i: (i // 2, i % 2, 0, 0)),
             pl.BlockSpec((1, HD), lambda i: (0, 0)),
         ],
         out_specs=(
             pl.BlockSpec((BAL, ROW, HD), lambda i: (0, 0, 0)),
             pl.BlockSpec((BAL, FEAT, ROW), lambda i: (0, 0, 0)),
-            pl.BlockSpec((FEAT, WIDE // 2), lambda i: (0, i)),
+            pl.BlockSpec((FEAT, GROUP), lambda i: (0, i)),
             pl.BlockSpec((1, HD), lambda i: (0, 0)),
         ),
         compiler_params=pltpu.CompilerParams(vmem_limit_bytes=56 * 1024 * 1024),

time: 122 us -> 120 us (0.984)
    pallas_call x1, Pallas kernels: 117 us -> 115 us  [main(): pl.pallas_call(main_kernel, out_shape=(jax.ShapeDtypeStruct((BAL, ROW, HD...]
where the time goes in v4:
time: 120 us
  Pallas kernels  119 us (99%)
    pallas_call x1, Pallas kernels, main(): pl.pallas_call(main_kernel, out_shape=(jax.ShapeDtypeStruct((BAL, ROW, HD...  115 us
    pallas_call x1, Pallas kernels, main(): pl.pallas_call(finish_kernel, grid=(4,), out_shape=(jax.ShapeDtypeStruct(...  4.34 us

profile of v4, /device:TPU:1, one launch (start us, length us, event | category | flops | bytes accessed | tf_op | source)
XLA Modules:
  0.0 120.1 jit_solution(17983332248271624233)
XLA Ops:
  0.6 115.2 %kv_grads.1 = (f32[3,128,128]{2,1,0:T(8,128)}, f32[3,320,128]{2,1,0:T(8,128)}, bf16[2,168,16,128]{3,2,1,0:T(8,128)(2,1)}, f32[1,128]{1,0:T(1,128)}) custom-call(s32[48]{0:T(128)} %counts.1, s32[48]{0:T(128)} %partner.1, bf16[4,320,128]{2,1,0:T(8,128)(2,1)} %bitcast.4, bf16[320,2048]{1,0:T(8,128)(2,1)} %w_hbm.1, f32[1,128]{1,0:T(1,128)} %bitcast.5, ...), custom_call_target="tpu_custom_call" | custom-call | tf_op jit(solution)/shard_map/kv_grads/pallas_call | solution.py:538
  115.8 4.3 %unpack.1 = (f32[3,128,128]{2,1,0:T(8,128)}, f32[3,320,128]{2,1,0:T(8,128)}, f32[320,2048]{1,0:T(8,128)}, f32[1,128]{1,0:T(1,128)}) custom-call(f32[3,128,128]{2,1,0:T(8,128)} %get-tuple-element.12.kv, f32[3,320,128]{2,1,0:T(8,128)} %get-tuple-element.13.rg, bf16[2,168,16,128]{3,2,1,0:T(8,128)(2,1)} %get-tuple-element.14.ag, f32[1,128]{1,0:T(1,128)} %get-tuple-element.15.gain), custom_call_target="tpu_custom_call" | custom-call | tf_op jit(solution)/shard_map/unpack/pallas_call | solution.py:592

commit v5 on v3

--- a/solution.py
+++ b/solution.py
@@ -188,19 +188,18 @@
                 hop_y(s, j)
 
     def first(j, hh):
-        return remote(offer.at[j], held.at[dp], first_s.at[hh, j], first_r.at[dp], mid_at(j, hh), t)
+        return remote(offer.at[j], held.at[dp], first_s.at[hh, j], first_r.at[dp], dp_at(j, hh, j % 2), t)
 
     def second(j, d):
         return remote(picked.at[d], moved.at[j], second_s.at[d], second_r.at[j], d, t)
 
     def each_mid(act):
-        @pl.loop(0, 2 * MIDS)
-        def _(n):
-            j, hh = n // 2, n % 2
-
-            @pl.when(dp != mid_at(j, hh))
-            def _():
-                act(j, hh)
+        for j in range(MIDS):
+            for hh in (0, 1):
+
+                @pl.when(dp != dp_at(j, hh, j % 2))
+                def _(j=j, hh=hh):
+                    act(j, hh)
 
     loads[0].wait()
     offer[...] = rows[jnp.clip(mine - 1, 0, CAP - 1)].reshape(MIDS, 2, 16, HD)
@@ -217,7 +216,6 @@
 
     loads[1].wait()
     send_x(0, jnp.where(0 < keep, rows[0], jnp.zeros((FEAT, ROW), BF16)))
-    send_x(2, jnp.where(2 < keep, rows[2], jnp.zeros((FEAT, ROW), BF16)))
 
     @pl.when(is_mid)
     def _():
@@ -235,6 +233,8 @@
             second(z, d).start()
 
         moved[z] = held[partner[dp]]
+
+    send_x(2, jnp.where(2 < keep, rows[2], jnp.zeros((FEAT, ROW), BF16)))
 
     is_key = t < KV
     gain = k_gain[...]
@@ -409,17 +409,21 @@
         )
 
     both = ((-1, 0), (1, 0), (-1, 1), (1, 1))
-    flat_first = sorted(both, key=lambda way: (deep(*way), way[1]))
-    for way in both:
-        pass_on(*way, 6 if deep(*way) else 5)
-    for way in both:
-        pass_on(*way, 4)
+    flat_first = sorted(both, key=lambda way: (way[1], deep(*way)))
+    for u in (0, 1):
+        for sign in (-1, 1):
+            pass_on(sign, u, 6 if deep(sign, u) else 5)
+        for sign in (-1, 1):
+            pass_on(sign, u, 4)
+        if u == 0:
+            for sign in (-1, 1):
+                pass_on(sign, u, 2)
     row_grad(ORDER[-1])
     for way in both:
         if deep(*way):
             pass_on(*way, 5)
-    for way in both:
-        pass_on(*way, 2)
+    for sign in (-1, 1):
+        pass_on(sign, 1, 2)
     for way in flat_first:
         pass_on(*way, 3)
     for way in flat_first:
@@ -508,7 +512,7 @@
 
 
 def finish_kernel(kv, rg, ag, gain, kv_out, rg_out, wg_out, gain_out):
-    for h in range(8):
+    for h in range(4):
         wg_out[:, h * HD : (h + 1) * HD] = ag[0, h * 20 : h * 20 + 20].reshape(FEAT, HD).astype(F32)
 
     @pl.when(pl.program_id(0) == 0)
@@ -578,7 +582,7 @@
     )(counts, partner, rows, w, k_gain, cot)
     return pl.pallas_call(
         finish_kernel,
-        grid=(2,),
+        grid=(4,),
         out_shape=(
             jax.ShapeDtypeStruct((BAL, ROW, HD), F32),
             jax.ShapeDtypeStruct((BAL, FEAT, ROW), F32),
@@ -588,13 +592,13 @@
         in_specs=[
             pl.BlockSpec((BAL, ROW, HD), lambda i: (0, 0, 0)),
             pl.BlockSpec((BAL, FEAT, ROW), lambda i: (0, 0, 0)),
-            pl.BlockSpec((1, NZ * TILES, 16, HD), lambda i: (i, 0, 0, 0)),
+            pl.BlockSpec((1, HALF_TILES // 2, 16, HD), lambda i: (i // 2, i % 2, 0, 0)),
             pl.BlockSpec((1, HD), lambda i: (0, 0)),
         ],
         out_specs=(
             pl.BlockSpec((BAL, ROW, HD), lambda i: (0, 0, 0)),
             pl.BlockSpec((BAL, FEAT, ROW), lambda i: (0, 0, 0)),
-            pl.BlockSpec((FEAT, WIDE // 2), lambda i: (0, i)),
+            pl.BlockSpec((FEAT, GROUP), lambda i: (0, i)),
             pl.BlockSpec((1, HD), lambda i: (0, 0)),
         ),
         compiler_params=pltpu.CompilerParams(vmem_limit_bytes=56 * 1024 * 1024),

time: 122 us -> 124 us (1.016)
  Pallas kernels: 120 us -> 123 us
    pallas_call x1, Pallas kernels: 117 us -> 119 us  [main(): pl.pallas_call(main_kernel, out_shape=(jax.ShapeDtypeStruct((BAL, ROW, HD...]
where the time goes in v5:
time: 124 us
  Pallas kernels  123 us (99%)
    pallas_call x1, Pallas kernels, main(): pl.pallas_call(main_kernel, out_shape=(jax.ShapeDtypeStruct((BAL, ROW, HD...  119 us
    pallas_call x1, Pallas kernels, main(): pl.pallas_call(finish_kernel, grid=(4,), out_shape=(jax.ShapeDtypeStruct(...  4.34 us

profile of v5, /device:TPU:1, one launch (start us, length us, event | category | flops | bytes accessed | tf_op | source)
XLA Modules:
  0.0 123.8 jit_solution(11188091451853762793)
XLA Ops:
  0.6 118.9 %kv_grads.1 = (f32[3,128,128]{2,1,0:T(8,128)}, f32[3,320,128]{2,1,0:T(8,128)}, bf16[2,168,16,128]{3,2,1,0:T(8,128)(2,1)}, f32[1,128]{1,0:T(1,128)}) custom-call(s32[48]{0:T(128)} %counts.1, s32[48]{0:T(128)} %partner.1, bf16[4,320,128]{2,1,0:T(8,128)(2,1)} %bitcast.4, bf16[320,2048]{1,0:T(8,128)(2,1)} %w_hbm.1, f32[1,128]{1,0:T(1,128)} %bitcast.5, ...), custom_call_target="tpu_custom_call" | custom-call | tf_op jit(solution)/shard_map/kv_grads/pallas_call | solution.py:531
  119.5 4.3 %unpack.1 = (f32[3,128,128]{2,1,0:T(8,128)}, f32[3,320,128]{2,1,0:T(8,128)}, f32[320,2048]{1,0:T(8,128)}, f32[1,128]{1,0:T(1,128)}) custom-call(f32[3,128,128]{2,1,0:T(8,128)} %get-tuple-element.12.kv, f32[3,320,128]{2,1,0:T(8,128)} %get-tuple-element.13.rg, bf16[2,168,16,128]{3,2,1,0:T(8,128)(2,1)} %get-tuple-element.14.ag, f32[1,128]{1,0:T(1,128)} %get-tuple-element.15.gain), custom_call_target="tpu_custom_call" | custom-call | tf_op jit(solution)/shard_map/unpack/pallas_call | solution.py:583
